TPU v7x, 32 devices: a whole 2x2x4 slice. The times are simulated.
32 devices in a mesh: rel: 4 (over z), ent: 8 (over y, x, core).
Axes of the slice: x: 2, y: 2, z: 4, core: 2. Of those that a mesh axis runs over, the one named last changes fastest.
Arguments:
- features: bfloat16 [4096, 512], P('ent'), may hold values from -6 to 6
- w_self: bfloat16 [512, 512], replicated, may hold values from -0.25 to 0.25
- basis_mats: bfloat16 [16384, 512], replicated, may hold values from -0.046875 to 0.046875
- basis_coeffs: float32 [1000, 32], replicated, may hold values from -5 to 5
- group_rels: int32 [1000], P('rel'), may hold values from 0 to 999, each once
- rel_local: int32 [16384], P(('rel', 'ent')), may hold values from 0 to 249
- edge_src: int32 [16384], P(('rel', 'ent')), may hold values from 0 to 4095, as said below
- edge_dst: int32 [16384], P(('rel', 'ent')), may hold values from 0 to 4095, as said below
- block_counts: int32 [4, 8, 8], P('rel', 'ent'), may hold values from 1 to 64, as said below
- cotangent: bfloat16 [4096, 512], P('ent'), may hold values from -6 to 6
Outputs:
- activations: bfloat16 [4096, 512], P('ent')
- grad_features: bfloat16 [4096, 512], P('ent')
- grad_basis: float32 [16384, 512], P(('rel', 'ent'))
Inputs may be any that keep to these rules, and one draw needn't show every extreme that they name: `edge_src`: slot i's source is owned by ent index (i // 512) % 8: it lies in [that index * 512, that index * 512 + 512). `edge_dst`: slot i's destination is owned by block index k = (i % 512) // 64: it lies in [k * 512, k * 512 + 512); within each aligned block of 64 slots the destinations are non-decreasing; the live slots of a block are its first block_counts ones. `block_counts`: one relation group, drawn from the seed, has every block full.
All inputs are finite; a program needn't handle non-finite values.
Results may differ from a plain program's by a relative error of at most 0.0059.
Values may be sent and summed in bfloat16 or wider, within the bound.
No kernel may reach another device: no remote copies, remote signals or barrier semaphores. Data moves between devices by JAX's collectives and lax.ppermute only.
A program may use at most 192 MiB of HBM per device.

v0:
```python
import jax
import jax.numpy as jnp
from jax import lax
from jax.sharding import PartitionSpec as P


def activate(features, w_self, partial_sums, in_degree, cotangent):
    inverse = 1.0 / jnp.maximum(in_degree, 1.0)
    pre_act = (
        jnp.dot(features, w_self, preferred_element_type=jnp.float32)
        + partial_sums * inverse[:, None]
    )
    sigmoid_pre = jax.nn.sigmoid(pre_act)
    out_rows = (pre_act * sigmoid_pre).astype(jnp.bfloat16)
    grad_pre = (
        cotangent.astype(jnp.float32) * (sigmoid_pre * (1.0 + pre_act * (1.0 - sigmoid_pre)))
    ).astype(jnp.bfloat16)
    grad_scaled = (grad_pre.astype(jnp.float32) * inverse[:, None]).astype(jnp.bfloat16)
    return (out_rows, grad_pre, grad_scaled)


def per_device(
    features,
    w_self,
    basis_mats,
    basis_coeffs,
    group_rels,
    rel_local,
    edge_src,
    edge_dst,
    block_counts,
    cotangent,
):
    ent_dev, feat_width = features.shape
    ent_count = lax.axis_size("ent")
    slot_count = rel_local.shape[0]
    block_cap = slot_count // ent_count
    basis_count = basis_coeffs.shape[1]
    first_row = lax.axis_index("ent") * ent_dev
    slot_index = jnp.arange(slot_count, dtype=jnp.int32)
    limits = jnp.repeat(block_counts.reshape(ent_count), block_cap, total_repeat_length=slot_count)
    is_live = slot_index % block_cap < limits
    rel_coef = basis_coeffs[group_rels[rel_local]]
    src_local = edge_src - first_row
    src_rows = features[src_local].astype(jnp.float32)
    mixed_rows = (
        (rel_coef[:, :, None] * src_rows[:, None, :])
        .reshape(slot_count, basis_count * feat_width)
        .astype(jnp.bfloat16)
    )
    product = jnp.dot(mixed_rows, basis_mats, preferred_element_type=jnp.float32)
    messages = (product * is_live.astype(jnp.float32)[:, None]).astype(jnp.bfloat16)
    owner_base = slot_index // block_cap * ent_dev
    targets = jnp.where(is_live, edge_dst - owner_base, ent_dev)
    arrived, dest_slots = (
        lax.all_to_all(
            messages.reshape(ent_count, block_cap, feat_width),
            "ent",
            split_axis=0,
            concat_axis=0,
            tiled=True,
        ),
        lax.all_to_all(
            targets.reshape(ent_count, block_cap), "ent", split_axis=0, concat_axis=0, tiled=True
        ),
    )
    arrived = arrived.reshape(slot_count, feat_width)
    dest_slots = dest_slots.reshape(slot_count)
    one_hot = (dest_slots[None, :] == jnp.arange(ent_dev, dtype=jnp.int32)[:, None]).astype(
        jnp.bfloat16
    )
    partial_sums = jnp.dot(one_hot, arrived, preferred_element_type=jnp.float32)
    in_degree = jnp.sum(one_hot, axis=1, dtype=jnp.float32)
    partial_sums, in_degree = lax.psum((partial_sums, in_degree), "rel")
    out_rows, grad_pre, grad_scaled = activate(features, w_self, partial_sums, in_degree, cotangent)
    picked = grad_scaled[jnp.minimum(dest_slots, ent_dev - 1)]
    grad_back = jnp.where((dest_slots < ent_dev)[:, None], picked, jnp.zeros((), jnp.bfloat16))
    returned = lax.all_to_all(
        grad_back.reshape(ent_count, block_cap, feat_width),
        "ent",
        split_axis=0,
        concat_axis=0,
        tiled=True,
    )
    returned = returned.reshape(slot_count, feat_width)
    grad_mixed = lax.dot_general(
        returned, basis_mats, (((1,), (1,)), ((), ())), preferred_element_type=jnp.float32
    )
    grad_rows = jnp.sum(
        grad_mixed.reshape(slot_count, basis_count, feat_width) * rel_coef[:, :, None], axis=1
    )
    grad_src = jax.ops.segment_sum(grad_rows, src_local, ent_dev)
    grad_src = lax.psum(grad_src, "rel")
    self_part = lax.dot_general(
        grad_pre, w_self, (((1,), (1,)), ((), ())), preferred_element_type=jnp.float32
    )
    grad_features = (self_part + grad_src).astype(jnp.bfloat16)
    grad_basis = lax.psum_scatter(
        lax.dot_general(
            mixed_rows, returned, (((0,), (0,)), ((), ())), preferred_element_type=jnp.float32
        ),
        ("rel", "ent"),
        scatter_dimension=0,
        tiled=True,
    )
    return (out_rows, grad_features, grad_basis)


def solution(mesh):
    placed = (
        P("ent", None),
        P(),
        P(),
        P(),
        P("rel"),
        P(("rel", "ent")),
        P(("rel", "ent")),
        P(("rel", "ent")),
        P("rel", "ent", None),
        P("ent", None),
    )
    return jax.shard_map(
        per_device,
        mesh=mesh,
        in_specs=placed,
        out_specs=(P("ent", None), P("ent", None), P(("rel", "ent"), None)),
        check_vma=False,
    )
```

profile of v0, /device:TPU:0, one launch (start us, length us, event | category | flops | bytes accessed | tf_op | source)
XLA Modules:
  0.0 592.2 jit_solution(12208384228441651072)
XLA Ops:
  7.2 1.6 fusion.17
  8.8 0.8 add_add_fusion.1
  9.6 4.4 compare_select_fusion.3
  14.0 1.4 fusion.11
  15.4 0.7 all_to_all.12
  16.1 5.2 all-to-all-start
  21.3 0.7 compare_select_fusion.10
  22.0 3.6 gather_fusion
  25.6 0.7 compare_select_fusion.9
  26.3 1.1 copy.25
  27.4 1.0 gather_fusion.1
  28.6 2.0 gather_fusion.2
  30.7 6.1 %multiply_convert_fusion = bf16[512,32,512]{2,0,1:T(8,128)(2,1)} fusion(f32[512,512]{1,0:T(8,128)S(1)} %convert_element_type.54, f32[512,32]{0,1:T(8,128)S(1)} %copy.26), kind=kLoop, calls=%fused_computation.6 | loop fusion | flops 16777216 | bytes 17891328 | tf_op jit(solution)/shard_map/convert_element_type | solution.py:49
  36.8 22.5 %copy.27 = bf16[512,32,512]{0,2,1:T(8,128)(2,1)} copy(bf16[512,32,512]{2,0,1:T(8,128)(2,1)} %multiply_convert_fusion) | data formatting | bytes 33554432 | tf_op jit(solution)/shard_map/convert_element_type | solution.py:49
  59.3 18.1 %fusion.1 = bf16[512,512]{1,0:T(8,128)(2,1)} fusion(bf16[512,16384]{0,1:T(8,128)(2,1)} %bitcast.46, bf16[16384,512]{1,0:T(8,128)(2,1)} %param.14, f32[512]{0:T(512)S(1)} %convert_element_type.57), kind=kOutput, calls=%fused_computation.11 | convolution fusion | flops 8590458880 | bytes 34080768 | tf_op jit(solution)/shard_map/dot_general | solution.py:51
  77.3 4.2 all-to-all-start.1
  81.6 0.5 broadcast.314
  82.1 0.7 minimum_reduce_fusion
  82.8 8.4 %all-to-all-done.1 = bf16[8,64,512]{2,1,0:T(8,128)(2,1)S(1)} async-done(((bf16[8,64,512]{2,1,0:T(8,128)(2,1)}), bf16[8,64,512]{2,1,0:T(8,128)(2,1)S(1)}, u32[]{:S(2)}, u32[]{:S(2)}) %all-to-all-start.1) | async-done | bytes 524320 | tf_op jit(solution)/shard_map/all_to_all | solution.py:56
  91.3 1.4 fusion.3
  93.0 12.1 %psum.22 = f32[512]{0:T(512)S(1)} all-reduce(f32[512]{0:T(512)S(1)} %convert_reduce_fusion), channel_id=1, replica_groups=mesh['rel'=4,'ent'=8] {'rel'}, use_global_device_ids=true, to_apply=%region_2.3 | all-reduce | flops 512 | bytes 4096 | tf_op jit(solution)/shard_map/psum | solution.py:74
  105.2 38.9 %all-reduce.3.cloned.1.call-done = f32[512,512]{1,0:T(8,128)} async-done(((f32[512,512]{1,0:T(8,128)}), f32[512,512]{1,0:T(8,128)}) %all-reduce.3.cloned.1.call-update) | async-done | bytes 1048592 | tf_op jit(solution)/shard_map/psum | solution.py:74
  144.1 2.9 multiply_convert_fusion.1
  147.0 2.0 gather_fusion.3
  149.1 13.2 %all_to_all.19 = bf16[8,64,512]{2,1,0:T(8,128)(2,1)S(1)} all-to-all(bf16[8,64,512]{2,1,0:T(8,128)(2,1)S(1)} %broadcast_select_fusion), channel_id=1, replica_groups=mesh['rel'=4,'ent'=8] {'ent'}, dimensions={0} | all-to-all | bytes 1048576 | tf_op jit(solution)/shard_map/all_to_all | solution.py:78
  162.3 12.6 %multiply_reduce_fusion = f32[512,512]{1,0:T(8,128)S(1)} fusion(f32[512,32]{0,1:T(8,128)S(1)} %copy.26, bf16[512,512,1]{1,0,2:T(8,128)(2,1)S(1)} %bitcast.50, bf16[32,512,512]{2,1,0:T(8,128)(2,1)} %bitcast.61), kind=kOutput, calls=%fused_computation.5 | convolution fusion | flops 8606449664 | bytes 18415616 | tf_op jit(solution)/shard_map/dot_general | solution.py:86
  175.0 4.6 scatter_custom_fusion
  179.6 0.3 reduce-scatter.2.cloned.1.call-start
  179.9 21.5 %fusion.18 = f32[16384,512]{1,0:T(8,128)} fusion(bf16[512,16384]{0,1:T(8,128)(2,1)} %bitcast.47, bf16[512,512]{1,0:T(8,128)(2,1)S(1)} %bitcast.51), kind=kOutput, calls=%fused_computation.64 | convolution fusion | flops 8589934592 | bytes 50855936 | tf_op jit(solution)/shard_map/dot_general | solution.py:99
  201.4 27.7 %all-reduce.5.cloned.1.call-done = f32[512,512]{1,0:T(8,128)} async-done(((f32[512,512]{1,0:T(8,128)}), f32[512,512]{1,0:T(8,128)}) %all-reduce.5.cloned.1.call-update) | async-done | bytes 1048592 | tf_op jit(solution)/shard_map/psum | solution.py:93
  229.1 2.5 fusion
  231.6 354.1 %reduce-scatter.2.cloned.1.call-done = f32[512,512]{1,0:T(8,128)} async-done(((f32[16384,512]{1,0:T(8,128)}), f32[512,512]{1,0:T(8,128)}) %reduce-scatter.2.cloned.1.call-update) | async-done | bytes 1048592 | tf_op jit(solution)/shard_map/reduce_scatter | solution.py:98
  (31 shorter events, 0.9 us)
Async XLA Ops:
  7.2 21.4 %copy-start = (bf16[512,512]{1,0:T(8,128)(2,1)S(1)}, bf16[512,512]{1,0:T(8,128)(2,1)}, u32[]{:S(2)}) copy-start(bf16[512,512]{1,0:T(8,128)(2,1)} %param.12) | copy-start | bytes 1572868
  16.1 61.2 %all-to-all-start = ((s32[8,1,64]{2,1,0:T(1,128)}), s32[8,1,64]{2,1,0:T(1,128)S(1)}, u32[]{:S(2)}, u32[]{:S(2)}) async-start(s32[8,1,64]{2,1,0:T(1,128)} %all_to_all.12), calls=%async_computation | async-start | bytes 8192 | tf_op jit(solution)/shard_map/all_to_all | solution.py:63
  59.3 84.9 %copy-start.2 = (bf16[512,512]{1,0:T(8,128)(2,1)S(1)}, bf16[512,512]{1,0:T(8,128)(2,1)}, u32[]{:S(2)}) copy-start(bf16[512,512]{1,0:T(8,128)(2,1)} %param.13) | copy-start | bytes 1572868
  59.3 84.9 %copy-start.3 = (bf16[512,512]{1,0:T(8,128)(2,1)S(1)}, bf16[512,512]{1,0:T(8,128)(2,1)}, u32[]{:S(2)}) copy-start(bf16[512,512]{1,0:T(8,128)(2,1)} %param.21) | copy-start | bytes 1572868
  77.3 13.9 %all-to-all-start.1 = ((bf16[8,64,512]{2,1,0:T(8,128)(2,1)}), bf16[8,64,512]{2,1,0:T(8,128)(2,1)S(1)}, u32[]{:S(2)}, u32[]{:S(2)}) async-start(bf16[8,64,512]{2,1,0:T(8,128)(2,1)} %bitcast.16), calls=%async_computation.1 | async-start | bytes 1048576 | tf_op jit(solution)/shard_map/all_to_all | solution.py:56
  81.5 62.6 %all-reduce.3.cloned.1.call-start = ((), (), s32[]{:S(2)}) async-start(), calls=%async_computation.4 | async-start | bytes 2097152 | tf_op jit(solution)/shard_map/psum | solution.py:74
  92.7 136.4 %all-reduce.5.cloned.1.call-start = ((), (), s32[]{:S(2)}) async-start(), calls=%async_computation.5 | async-start | bytes 2097152 | tf_op jit(solution)/shard_map/psum | solution.py:93
  179.6 406.1 %reduce-scatter.2.cloned.1.call-start = ((), (), s32[]{:S(2)}) async-start(), calls=%async_computation.6 | async-start | bytes 34603008 | tf_op jit(solution)/shard_map/reduce_scatter | solution.py:98
  201.4 384.3 %copy-start.1 = (bf16[512,512]{1,0:T(8,128)(2,1)S(1)}, bf16[512,512]{1,0:T(8,128)(2,1)}, u32[]{:S(2)}) copy-start(bf16[512,512]{1,0:T(8,128)(2,1)} %param.12) | copy-start | bytes 1572868
Sparse Core Ops, SparseCore 0:
  92.8 51.2 all-reduce.2
  179.7 49.3 all-reduce.4
  232.0 353.6 reduce-scatter.1
where the time goes:
time: 598 us; the launch traced here: 592 us
  waiting for transfers between devices  429 us (72%)
  matrix products  59 us (10%)
  local copies, waits for them, and re-layouts  35.3 us (6%)
  blocking collectives  25.3 us (4%)
  other arithmetic  19.8 us (3%)
  between operations  13.9 us (2%)
  starting transfers between devices  9.71 us (2%)
    reduce_scatter x1, waiting for transfers between devices, per_device(): lax.psum_scatter(lax.dot_general(mixed_rows, returned, (((0,), (0,)), (()...  354 us
    psum x1, waiting for transfers between devices, per_device(): partial_sums, in_degree = lax.psum((partial_sums, in_degree), 'rel')  38.9 us
    psum x1, waiting for transfers between devices, per_device(): grad_src = lax.psum(grad_src, 'rel')  27.7 us
    convert_element_type x1, local copies, waits for them, and re-layouts, per_device(): mixed_rows = (rel_coef[:, :, None] * src_rows[:, None, :]).reshape(slot_c...  22.5 us
    dot_general x1, matrix products, per_device(): lax.dot_general(mixed_rows, returned, (((0,), (0,)), ((), ())), preferred...  21.5 us
    dot_general x1, matrix products, per_device(): jnp.dot(mixed_rows, basis_mats, preferred_element_type=jnp.float32)  18.1 us
    all_to_all x1, blocking collectives, per_device(): lax.all_to_all(grad_back.reshape(ent_count, block_cap, feat_width), 'ent'...  13.2 us
    dot_general x1, matrix products, per_device(): lax.dot_general(returned, basis_mats, (((1,), (1,)), ((), ())), preferred...  12.6 us
  transfers between devices with their start and end apart: 5, of which 4 were waited for; matrix products, arithmetic and copies ran while one was open for 14% of the time, Pallas kernels for 0%

commit v1 on v0

v1 whole, which is shorter than its diff:
```python
import functools

import jax
import jax.numpy as jnp
from jax import lax
from jax.experimental import pallas as pl
from jax.experimental.pallas import tpu as pltpu
from jax.sharding import PartitionSpec as P

BF = jnp.bfloat16
F32 = jnp.float32
VMEM = pl.BlockSpec(memory_space=pltpu.VMEM)
SMEM = pl.BlockSpec(memory_space=pltpu.SMEM)
VMEM_LIMIT = 56 * 1024 * 1024
Z_SPLIT = 2
TABLE = 256


def dot(a, b):
    return jnp.dot(a, b, preferred_element_type=F32)


def dot_nt(a, b):
    return lax.dot_general(a, b, (((1,), (1,)), ((), ())), preferred_element_type=F32)


def one_hot(row, count):
    places = lax.broadcasted_iota(jnp.int32, (count, row.shape[1]), 0)
    return jnp.where(places == row, 1.0, 0.0).astype(BF)


def split3(x):
    high = x.astype(BF)
    rest = x - high.astype(F32)
    middle = rest.astype(BF)
    return high, middle, (rest - middle.astype(F32)).astype(BF)


def call(kernel, outs, ins, *args, scratch=(), flops=0, **more):
    size = sum(a.size * a.dtype.itemsize for a in args) + sum(o.size * o.dtype.itemsize for o in outs)
    return pl.pallas_call(
        kernel,
        out_shape=tuple(outs),
        in_specs=ins,
        out_specs=tuple(VMEM for _ in outs),
        scratch_shapes=scratch,
        compiler_params=pltpu.CompilerParams(vmem_limit_bytes=VMEM_LIMIT),
        cost_estimate=pl.CostEstimate(flops=flops, bytes_accessed=size, transcendentals=0),
        **more,
    )(*args)


def transpose_kernel(h_ref, in_ref, out_ref):
    out_ref[0] = in_ref[0].T


def transposed_columns(basis, half, cols):
    count, depth, _ = basis.shape
    return pl.pallas_call(
        transpose_kernel,
        grid_spec=pltpu.PrefetchScalarGridSpec(
            num_scalar_prefetch=1,
            grid=(count,),
            in_specs=[pl.BlockSpec((1, depth, cols), lambda i, h: (i, 0, h[0]))],
            out_specs=pl.BlockSpec((1, cols, depth), lambda i, h: (i, 0, 0)),
        ),
        out_shape=jax.ShapeDtypeStruct((count, cols, depth), BF),
        cost_estimate=pl.CostEstimate(flops=0, bytes_accessed=4 * count * cols * depth, transcendentals=0),
    )(half, basis)


def prep_kernel(pos_ref, meta_ref, coeffs_ref, slots_ref, coef_in_ref, coef_out_ref, coef_b_ref,
                table_ref, pieces_ref, own_ref, *, n_rel, n_ent):
    ent, own_basis = pos_ref[0], pos_ref[1]
    basis_count = coeffs_ref.shape[0]
    cap = meta_ref.shape[2] // n_ent
    lanes = n_rel * cap
    n_high = n_rel * TABLE // 128

    coeff3 = jnp.concatenate(split3(coeffs_ref[...]), axis=0)
    for g in range(n_rel):
        picks = one_hot(meta_ref[g * n_ent, 3:4, :TABLE], coeffs_ref.shape[1])
        got = dot(coeff3, picks)
        rows = got[:basis_count] + got[basis_count:2 * basis_count] + got[2 * basis_count:]
        for part in range(TABLE // 128):
            table_ref[g * (TABLE // 128) + part] = rows[:, part * 128:(part + 1) * 128]
    for i, piece in enumerate(split3(table_ref[...].reshape(n_high * basis_count, 128))):
        pieces_ref[pl.ds(i * n_high * basis_count, n_high * basis_count), :] = piece
    own_row = table_ref[:, pl.ds(own_basis, 1), :].reshape(n_high, 128)
    pad = jnp.zeros((16 - n_high, 128), F32) if n_high < 16 else None
    own_rows = own_row if pad is None else jnp.concatenate([own_row, pad], axis=0)
    own_ref[...] = jnp.concatenate(split3(own_rows), axis=0)

    def regroup(s, carry):
        for g in range(n_rel):
            block = meta_ref[g * n_ent + s]
            for k in range(n_ent):
                slots_ref[s, k, :, g * cap:(g + 1) * cap] = block[:, k * cap:(k + 1) * cap]
        return carry

    lax.fori_loop(0, n_ent, regroup, 0)
    group = lax.broadcasted_iota(jnp.int32, (1, lanes), 1) // cap

    def low_high(s, k):
        index = group * TABLE + slots_ref[s, k, 0:1, :]
        return one_hot(index % 128, 128), index // 128

    def every(s, k):
        low, high = low_high(s, k)
        got = dot(pieces_ref[...], low)
        n = n_high * basis_count
        got = got[:n] + got[n:2 * n] + got[2 * n:]
        total = jnp.zeros((basis_count, lanes), F32)
        for i in range(n_high):
            total += jnp.where(high == i, got[i * basis_count:(i + 1) * basis_count], 0.0)
        return total

    def ends(m, carry):
        coef_in_ref[m] = every(ent ^ m, ent)
        coef_out_ref[m] = every(ent, ent ^ m)
        return carry

    lax.fori_loop(0, n_ent, ends, 0)
    n_own = own_rows.shape[0]

    def pairs(i, carry):
        s = i // n_ent
        k = i % n_ent
        low, high = low_high(s, k)
        got = dot(own_ref[...], low)
        got = got[:n_own] + got[n_own:2 * n_own] + got[2 * n_own:]
        mine = lax.broadcasted_iota(jnp.int32, got.shape, 0) == high
        coef_b_ref[s, k] = jnp.sum(jnp.where(mine, got, 0.0), axis=0, keepdims=True)
        return carry

    lax.fori_loop(0, n_ent * n_ent, pairs, 0)


def gather_chunks(refs, layout, out_ref):
    if layout is None:
        return refs[0]
    at = 0
    for m, parts in enumerate(layout):
        row = 0
        for rows in parts:
            out_ref[m, row:row + rows, :] = refs[at][...]
            row, at = row + rows, at + 1
    return out_ref


def chunk_scratch(layout, n_ent, depth, ents):
    return pltpu.VMEM((1, 8, 128) if layout is None else (n_ent, depth, ents), BF)


def weighted(weights_ref, coef_ref, m, columns, acc_ref, group):
    basis_count, cols, depth = weights_ref.shape
    acc_ref[...] = jnp.zeros_like(acc_ref)
    for first in range(0, basis_count, group):
        got = dot(weights_ref[first:first + group].reshape(group * cols, depth), columns)
        part = got[:cols] * coef_ref[m, first:first + 1, :]
        for i in range(1, group):
            part += got[i * cols:(i + 1) * cols] * coef_ref[m, first + i:first + i + 1, :]
        acc_ref[...] += part


def forward_kernel(*refs, layout, n_ent, half_axis):
    n_parts = sum(len(p) for p in layout) if layout else 1
    (pos_ref, slots_ref, coef_ref, weights_ref, wself_ref, cot_ref) = refs[:6]
    chunk_refs = refs[6:6 + n_parts]
    out_ref, grad_ref = refs[6 + n_parts:8 + n_parts]
    feat_ref, acc_ref, msg_ref, hot_ref = refs[8 + n_parts:]
    ent = pos_ref[0]
    cols = weights_ref.shape[1]
    lanes = slots_ref.shape[3]
    feat_ref = gather_chunks(chunk_refs, layout, feat_ref)
    ents = feat_ref.shape[2]
    msg_ref[:, cols:, :] = jnp.ones((n_ent, msg_ref.shape[1] - cols, lanes), BF)

    def sender(m, carry):
        s = ent ^ m
        picked = dot(feat_ref[m], one_hot(slots_ref[s, ent, 1:2, :], ents)).astype(BF)
        weighted(weights_ref, coef_ref, m, picked, acc_ref, 1024 // cols)
        msg_ref[m, :cols, :] = acc_ref[...].astype(BF)
        hot_ref[m] = one_hot(slots_ref[s, ent, 2:3, :], ents)
        return carry

    lax.fori_loop(0, n_ent, sender, 0)
    sums = dot_nt(msg_ref[0], hot_ref[0])
    for m in range(1, n_ent):
        sums += dot_nt(msg_ref[m], hot_ref[m])
    inverse = 1.0 / jnp.maximum(sums[cols:cols + 1, :], 1.0)
    pre = dot(wself_ref[...], feat_ref[0]) + sums[:cols] * inverse
    sig = jax.nn.sigmoid(pre)
    out_ref[...] = (pre * sig).T.astype(BF)
    grad_ref[...] = (cot_ref[...].astype(F32) * (sig * (1.0 + pre * (1.0 - sig)))).astype(BF)


def scatter_kernel(*refs, layout, n_ent, rows):
    n_parts = sum(len(p) for p in layout) if layout else 1
    pos_ref, slots_ref, coef_ref = refs[:3]
    chunk_refs = refs[3:3 + n_parts]
    mix_out_ref, degree_ref = refs[3 + n_parts:5 + n_parts]
    feat_ref, mix_ref, hot_ref = refs[5 + n_parts:]
    ent = pos_ref[0]
    lanes = slots_ref.shape[3]
    feat_ref = gather_chunks(chunk_refs, layout, feat_ref)
    ents = feat_ref.shape[2]
    mix_ref[:, rows:, :] = jnp.ones((n_ent, mix_ref.shape[1] - rows, lanes), BF)
    first = pl.multiple_of(pos_ref[2], 128)

    def receiver(n, carry):
        k = ent ^ n

        for m in range(n_ent):
            s = ent ^ m
            hot = one_hot(slots_ref[s, k, 1:2, :], ents)
            got = dot(feat_ref[m, pl.ds(first, rows), :], hot)
            mix_ref[m, :rows, :] = (got * coef_ref[s, k]).astype(BF)
            hot_ref[m] = one_hot(slots_ref[s, k, 2:3, :], ents)
        total = dot_nt(mix_ref[0], hot_ref[0])
        for m in range(1, n_ent):
            total += dot_nt(mix_ref[m], hot_ref[m])
        mix_out_ref[n] = total[:rows].astype(BF)
        degree_ref[n] = total[rows:rows + 8]
        return carry

    lax.fori_loop(0, n_ent, receiver, 0)


def backward_kernel(*refs, layout, n_ent, basis_shape):
    n_parts = sum(len(p) for p in layout) if layout else 1
    (pos_ref, slots_ref, coef_ref, weights_ref, wself_ref, degree_ref) = refs[:6]
    chunk_refs = refs[6:6 + n_parts]
    out_ref, scaled_out_ref = refs[6 + n_parts:8 + n_parts]
    grad_ref, acc_ref, row_ref, hot_ref = refs[8 + n_parts:]
    ent = pos_ref[0]
    cols = weights_ref.shape[1]
    grad_ref = gather_chunks(chunk_refs, layout, grad_ref)
    ents = grad_ref.shape[2]
    self_part = dot(wself_ref[...], grad_ref[0])

    def receiver(n, carry):
        k = ent ^ n
        inverse = 1.0 / jnp.maximum(degree_ref[n, 0:1, :], 1.0)
        scaled = (grad_ref[n].astype(F32) * inverse).astype(BF)
        scaled_out_ref[n] = scaled
        picked = dot(scaled, one_hot(slots_ref[ent, k, 2:3, :], ents)).astype(BF)
        weighted(weights_ref, coef_ref, n, picked, acc_ref, 1024 // cols)
        total = acc_ref[...]
        high = total.astype(BF)
        row_ref[n, :cols, :] = high
        row_ref[n, cols:, :] = (total - high.astype(F32)).astype(BF)
        hot_ref[n] = one_hot(slots_ref[ent, k, 1:2, :], ents)
        return carry

    lax.fori_loop(0, n_ent, receiver, 0)
    sums = dot_nt(row_ref[0], hot_ref[0])
    for n in range(1, n_ent):
        sums += dot_nt(row_ref[n], hot_ref[n])
    out_ref[...] = (self_part + sums[:cols] + sums[cols:]).T.astype(BF)


def basis_kernel(mix_ref, scaled_ref, out_ref):
    total = dot_nt(mix_ref[0], scaled_ref[0])
    for n in range(1, mix_ref.shape[0]):
        total += dot_nt(mix_ref[n], scaled_ref[n])
    out_ref[...] = total


def exchange(x, mask, axis):
    count = lax.axis_size(axis)
    return lax.ppermute(x, axis, [(i, i ^ mask) for i in range(count)])


def plane_chunks(x):
    n_ent = lax.axis_size("ent")
    rows = x.shape[0]
    if n_ent == 8:
        a, b = exchange(x, 2, "ent"), exchange(x, 4, "ent")
        c = exchange(x, 1, "ent")
        top = exchange(b[:rows // 2], 2, "ent")
        low = exchange(a[rows // 2:], 4, "ent")
        ca, cb = exchange(a, 1, "ent"), exchange(b, 1, "ent")
        c_top, c_low = exchange(top, 1, "ent"), exchange(low, 1, "ent")
        return [[x], [c], [a], [ca], [b], [cb], [top, low], [c_top, c_low]]
    whole = lax.all_gather(x, "ent", axis=0)
    order = lax.axis_index("ent") ^ jnp.arange(n_ent, dtype=jnp.int32)
    return whole[order]


def flat(chunks):
    if not isinstance(chunks, list):
        return [chunks], None
    return [p for parts in chunks for p in parts], [[p.shape[0] for p in parts] for parts in chunks]


def join(own, half, split, axis):
    pieces = [own] + [exchange(own, m, "rel") for m in range(1, split)]
    if split == 1:
        return own
    if split == 2:
        swap = half == 1
        return jnp.concatenate(
            [jnp.where(swap, pieces[1], pieces[0]), jnp.where(swap, pieces[0], pieces[1])], axis=axis
        )
    size = own.shape[axis]
    shape = list(own.shape)
    shape[axis] = size * split
    whole = jnp.zeros(shape, own.dtype)
    for m, piece in enumerate(pieces):
        whole = lax.dynamic_update_slice_in_dim(whole, piece, (half ^ m) * size, axis)
    return whole


def per_device(features, w_self, basis_mats, basis_coeffs, group_rels, rel_local, edge_src,
               edge_dst, block_counts, cotangent):
    ents, depth = features.shape
    n_ent, n_rel = lax.axis_size("ent"), lax.axis_size("rel")
    ent, rel = lax.axis_index("ent"), lax.axis_index("rel")
    slots = rel_local.shape[0]
    cap = slots // n_ent
    lanes = n_rel * cap
    n_rels, basis_count = basis_coeffs.shape
    rows = basis_count * depth // (n_ent * n_rel)
    split = Z_SPLIT if n_rel % Z_SPLIT == 0 else 1
    cols = depth // split
    half = rel % split
    place = rel * n_ent + ent

    index = jnp.arange(slots, dtype=jnp.int32)
    limits = jnp.repeat(block_counts.reshape(n_ent), cap, total_repeat_length=slots)
    target = jnp.where(index % cap < limits, edge_dst - index // cap * ents, -1)
    meta = jnp.stack([
        rel_local,
        edge_src - ent * ents,
        target,
        jnp.pad(group_rels, (0, slots - group_rels.shape[0]), constant_values=-1),
    ])
    meta = lax.all_to_all(
        jnp.broadcast_to(meta[None], (n_rel * n_ent, 4, slots)), ("rel", "ent"), 0, 0, tiled=True
    )
    feat, feat_layout = flat(plane_chunks(features.T))

    first_row = place * rows
    pos = jnp.stack([ent, first_row // depth, first_row % depth]).astype(jnp.int32)
    half_arr = half.reshape(1).astype(jnp.int32)
    basis = basis_mats.reshape(basis_count, depth, depth)
    columns = transposed_columns(basis, half_arr, cols)
    own_rows = lax.dynamic_slice_in_dim(basis, half * cols, cols, axis=1)
    wself_t = lax.dynamic_slice_in_dim(w_self, half * cols, cols, axis=1).T
    wself_rows = lax.dynamic_slice_in_dim(w_self, half * cols, cols, axis=0)
    cot_t = lax.dynamic_slice_in_dim(cotangent, half * cols, cols, axis=1).T
    padded = -(-n_rels // 128) * 128
    coeffs_t = jnp.pad(basis_coeffs, ((0, padded - n_rels), (0, 0))).T

    n_high = n_rel * TABLE // 128
    per_end = jax.ShapeDtypeStruct((n_ent, basis_count, lanes), F32)
    grouped, coef_in, coef_out, coef_b = call(
        functools.partial(prep_kernel, n_rel=n_rel, n_ent=n_ent),
        [
            jax.ShapeDtypeStruct((n_ent, n_ent, 4, lanes), jnp.int32),
            per_end,
            per_end,
            jax.ShapeDtypeStruct((n_ent, n_ent, 1, lanes), F32),
        ],
        [SMEM, VMEM, VMEM],
        pos, meta, coeffs_t,
        scratch=[
            pltpu.VMEM((n_high, basis_count, 128), F32),
            pltpu.VMEM((3 * n_high * basis_count, 128), BF),
            pltpu.VMEM((3 * max(16, n_high), 128), BF),
        ],
        flops=10**9,
    )

    out_cols, grad_cols = call(
        functools.partial(forward_kernel, layout=feat_layout, n_ent=n_ent, half_axis=None),
        [jax.ShapeDtypeStruct((ents, cols), BF), jax.ShapeDtypeStruct((cols, ents), BF)],
        [SMEM] + [VMEM] * (5 + len(feat)),
        pos, grouped, coef_in, columns, wself_t, cot_t, *feat,
        scratch=[
            chunk_scratch(feat_layout, n_ent, depth, ents),
            pltpu.VMEM((cols, lanes), F32),
            pltpu.VMEM((n_ent, cols + 16, lanes), BF),
            pltpu.VMEM((n_ent, ents, lanes), BF),
        ],
        flops=2 * n_ent * lanes * basis_count * depth * cols,
    )
    grad_pre = join(grad_cols, half, split, 0)
    grads, grad_layout = flat(plane_chunks(grad_pre))

    mixed, degree = call(
        functools.partial(scatter_kernel, layout=feat_layout, n_ent=n_ent, rows=rows),
        [jax.ShapeDtypeStruct((n_ent, rows, ents), BF), jax.ShapeDtypeStruct((n_ent, 8, ents), F32)],
        [SMEM] + [VMEM] * (2 + len(feat)),
        pos, grouped, coef_b, *feat,
        scratch=[
            chunk_scratch(feat_layout, n_ent, depth, ents),
            pltpu.VMEM((n_ent, rows + 16, lanes), BF),
            pltpu.VMEM((n_ent, ents, lanes), BF),
        ],
        flops=4 * n_ent * n_ent * lanes * rows * ents,
    )

    grad_out, scaled = call(
        functools.partial(backward_kernel, layout=grad_layout, n_ent=n_ent, basis_shape=None),
        [jax.ShapeDtypeStruct((ents, cols), BF), jax.ShapeDtypeStruct((n_ent, depth, ents), BF)],
        [SMEM] + [VMEM] * (5 + len(grads)),
        pos, grouped, coef_out, own_rows, wself_rows, degree, *grads,
        scratch=[
            chunk_scratch(grad_layout, n_ent, depth, ents),
            pltpu.VMEM((cols, lanes), F32),
            pltpu.VMEM((n_ent, 2 * cols, lanes), BF),
            pltpu.VMEM((n_ent, ents, lanes), BF),
        ],
        flops=2 * n_ent * lanes * basis_count * depth * cols,
    )
    grad_features = join(grad_out, half, split, 1)
    activations = join(out_cols, half, split, 1)
    (grad_basis,) = call(
        basis_kernel,
        [jax.ShapeDtypeStruct((rows, depth), F32)],
        [VMEM, VMEM],
        mixed, scaled,
        flops=2 * n_ent * rows * ents * depth,
    )
    return activations, grad_features, grad_basis


def solution(mesh):
    placed = (
        P("ent", None),
        P(),
        P(),
        P(),
        P("rel"),
        P(("rel", "ent")),
        P(("rel", "ent")),
        P(("rel", "ent")),
        P("rel", "ent", None),
        P("ent", None),
    )
    return jax.shard_map(
        per_device,
        mesh=mesh,
        in_specs=placed,
        out_specs=(P("ent", None), P("ent", None), P(("rel", "ent"), None)),
        check_vma=False,
    )
```

time: 598 us -> 203 us (0.34)
  waiting for transfers between devices: 429 us -> 25.4 us
  Pallas kernels: 0 us -> 124 us
  matrix products: 59 us -> 0 us
  blocking collectives: 25.3 us -> 0 us
  local copies, waits for them, and re-layouts: 35.3 us -> 19 us
  between operations: 13.9 us -> 0.93 us
  starting transfers between devices: 9.71 us -> 21.3 us
  other arithmetic: 19.8 us -> 11.4 us
    reduce_scatter x1 -> x0, waiting for transfers between devices: 354 us -> none  [per_device(): lax.psum_scatter(lax.dot_general(mixed_rows, returned, (((0,), (0,)), (()...]
    pallas_call x0 -> x6, Pallas kernels: none -> 124 us  [the longest x5 104 us: call(): pl.pallas_call(kernel, out_shape=tuple(outs), in_specs=ins, out_specs=tup...]
    psum x2 -> x0, waiting for transfers between devices: 66.6 us -> none  [the longest x1 38.9 us: per_device(): partial_sums, in_degree = lax.psum((partial_sums, in_degree), 'rel')]
    dot_general x6 -> x0, matrix products: 59 us -> none  [the longest x1 21.5 us: per_device(): lax.dot_general(mixed_rows, returned, (((0,), (0,)), ((), ())), preferred...]
    ppermute x0 -> x21, waiting for transfers between devices: none -> 25.4 us  [exchange(): return lax.ppermute(x, axis, [(i, i ^ mask) for i in range(count)])]
    convert_element_type x1 -> x0, local copies, waits for them, and re-layouts: 22.5 us -> none  [per_device(): mixed_rows = (rel_coef[:, :, None] * src_rows[:, None, :]).reshape(slot_c...]
    ppermute x0 -> x21, starting transfers between devices: none -> 17.3 us  [exchange(): return lax.ppermute(x, axis, [(i, i ^ mask) for i in range(count)])]
    all_to_all x1 -> x0, blocking collectives: 13.2 us -> none  [per_device(): lax.all_to_all(grad_back.reshape(ent_count, block_cap, feat_width), 'ent'...]
  transfers between devices with their start and end apart: 5 -> 22, of which waited for: 4 -> 4; matrix products, arithmetic and copies ran while one was open for 14% -> 12% of each run, Pallas kernels for 0% -> 34%
where the time goes in v1:
time: 203 us; the launch traced here: 202 us
  Pallas kernels  124 us (61%)
  waiting for transfers between devices  25.4 us (13%)
  starting transfers between devices  21.3 us (10%)
  local copies, waits for them, and re-layouts  19 us (9%)
  other arithmetic  11.4 us (6%)
    pallas_call x5, Pallas kernels, call(): pl.pallas_call(kernel, out_shape=tuple(outs), in_specs=ins, out_specs=tup...  104 us
    ppermute x21, waiting for transfers between devices, exchange(): return lax.ppermute(x, axis, [(i, i ^ mask) for i in range(count)])  25.4 us
    pallas_call x1, Pallas kernels, transposed_columns(): pl.pallas_call(transpose_kernel, grid_spec=pltpu.PrefetchScalarGridSpec(n...  20.5 us
    ppermute x21, starting transfers between devices, exchange(): return lax.ppermute(x, axis, [(i, i ^ mask) for i in range(count)])  17.3 us
    dynamic_slice x1, local copies, waits for them, and re-layouts, per_device(): own_rows = lax.dynamic_slice_in_dim(basis, half * cols, cols, axis=1)  7.56 us
    unnamed x45, local copies, waits for them, and re-layouts  5.84 us
    gather x2, other arithmetic, per_device(): jnp.repeat(block_counts.reshape(n_ent), cap, total_repeat_length=slots)  4.44 us
  transfers between devices with their start and end apart: 22, of which 4 were waited for; matrix products, arithmetic and copies ran while one was open for 12% of the time, Pallas kernels for 34%

profile of v1, /device:TPU:0, one launch (start us, length us, event | category | flops | bytes accessed | tf_op | source)
XLA Modules:
  0.0 202.2 jit_solution(10325735149613791231)
XLA Ops:
  0.6 1.3 copy.15
  1.9 3.0 %collective-permute-start.3 = (bf16[512,512]{1,0:T(8,128)(2,1)S(1)}, bf16[512,512]{1,0:T(8,128)(2,1)S(1)}, u32[]{:S(2)}, u32[]{:S(2)}) collective-permute-start(bf16[512,512]{1,0:T(8,128)(2,1)S(1)} %bitcast.35), channel_id=1, source_target_pairs={{0,4},{1,5},{2,6},{3,7},{4,0},{5,1},{6,2},{7,3},{8,12},{9,13},{10,... | collective-permute-start | bytes 1572872 | tf_op jit(solution)/shard_map/ppermute | solution.py:272
  4.9 1.5 collective-permute-start.1
  6.4 1.6 fusion.9
  9.5 4.4 %compare_select_fusion.1 = s32[512,1]{0,1:T(1,128)S(1)} fusion(s32[]{:T(128)} %bitcast.10, s32[]{:T(128)} %bitcast.11, s32[]{:T(128)} %bitcast.12, s32[]{:T(128)} %bitcast.13, s32[]{:T(128)} %bitcast.14, s32[]{:T(128)} %bitcast.16, s32[]{:T(128)} %bitcast.15, s32[512,1]{0,1:T(1,128)S(1)} %bitcast.45, s32[512,1]{0,1:T(1,128)S(1)} %bitcast.43), kind=kLoop, calls=%fused_computation.13 | loop fusion | flops 7168 | bytes 6172 | tf_op jit(solution)/shard_map/jit(_take)/gather | solution.py:331
  14.6 1.4 fusion.4
  17.5 4.0 %all-to-all-start = ((s32[32,4,512]{2,1,0:T(4,128)}), s32[32,4,512]{2,1,0:T(4,128)S(1)}, u32[]{:S(2)}, u32[]{:S(2)}) async-start(s32[32,4,512]{2,1,0:T(4,128)} %broadcast_in_dim.11), calls=%async_computation | async-start | bytes 524288 | tf_op jit(solution)/shard_map/all_to_all | solution.py:339
  21.5 1.8 collective-permute-start.5
  23.3 1.5 collective-permute-start.6
  25.4 1.1 constant_dynamic-slice_fusion.2
  26.4 6.4 %collective-permute-done.5.refs_12_.refs_9_ = bf16[256,512]{1,0:T(8,128)(2,1)} collective-permute-done((bf16[256,512]{1,0:T(8,128)(2,1)S(1)}, bf16[256,512]{1,0:T(8,128)(2,1)}, u32[]{:S(2)}, u32[]{:S(2)}) %collective-permute-start.5) | collective-permute-done | bytes 262176 | tf_op jit(solution)/shard_map/ppermute | solution.py:272
  32.8 0.8 collective-permute-done.6.refs_13_.refs_10_
  34.2 0.8 copy.16
  35.0 0.9 copy.17
  35.9 20.5 %shard_map.122.refs_3_ = bf16[32,256,512]{2,1,0:T(8,128)(2,1)} custom-call(s32[1]{0:T(128)} %bitcast.21.h_ref, bf16[32,512,512]{2,1,0:T(8,128)(2,1)} %bitcast.33), custom_call_target="tpu_custom_call" | custom-call | bytes 16777216 | tf_op jit(solution)/shard_map/pallas_call | solution.py:59
  57.8 16.8 %shard_map.121 = (s32[8,8,4,256]{3,2,1,0:T(4,128)}, f32[8,32,256]{2,1,0:T(8,128)}, f32[8,32,256]{2,1,0:T(8,128)}, f32[8,8,1,256]{3,2,1,0:T(1,128)}) custom-call(s32[3]{0:T(128)} %pad_add_fusion.1.pos_ref.refs_0_, s32[32,4,512]{2,1,0:T(4,128)} %copy-done.3, f32[32,1024]{1,0:T(8,128)} %pad_bitcast_fusion.coeffs_ref), custom_call_target="tpu_custom_call" | custom-call | flops 1000000000 | bytes 1245196 | tf_op jit(solution)/shard_map/pallas_call | solution.py:41
  75.6 27.7 %shard_map.123 = (bf16[512,256]{1,0:T(8,128)(2,1)}, bf16[256,512]{1,0:T(8,128)(2,1)}) custom-call(s32[3]{0:T(128)} %pad_add_fusion.1.pos_ref.refs_0_, s32[8,8,4,256]{3,2,1,0:T(4,128)} %get-tuple-element.25.refs_1_, f32[8,32,256]{2,1,0:T(8,128)} %get-tuple-element.26.refs_2_, bf16[32,256,512]{2,1,0:T(8,128)(2,1)} %shard_map.122.refs_3_, ...), custom_call_target="tpu_custom_call" | custom-call | flops 17179869184 | bytes 14155788 | tf_op jit(solution)/shard_map/pallas_call | solution.py:41
  103.3 1.4 collective-permute-start.10
  104.7 7.5 %collective-permute-done.10 = bf16[256,512]{1,0:T(8,128)(2,1)S(1)} collective-permute-done((bf16[256,512]{1,0:T(8,128)(2,1)}, bf16[256,512]{1,0:T(8,128)(2,1)S(1)}, u32[]{:S(2)}, u32[]{:S(2)}) %collective-permute-start.10) | collective-permute-done | bytes 262176 | tf_op jit(solution)/shard_map/ppermute | solution.py:272
  112.2 1.0 broadcast_select_fusion.1
  113.3 1.0 collective-permute-start.14
  115.0 1.2 collective-permute-start.9
  116.3 10.6 %collective-permute-done.14.refs_10_ = bf16[512,512]{1,0:T(8,128)(2,1)S(1)} collective-permute-done((bf16[512,512]{1,0:T(8,128)(2,1)S(1)}, bf16[512,512]{1,0:T(8,128)(2,1)S(1)}, u32[]{:S(2)}, u32[]{:S(2)}) %collective-permute-start.14) | collective-permute-done | bytes 524320 | tf_op jit(solution)/shard_map/ppermute | solution.py:272
  126.9 0.9 collective-permute-start.16
  127.9 0.9 collective-permute-start.17
  128.8 7.6 %constant_dynamic-slice_fusion.1.refs_3_ = bf16[32,256,512]{2,1,0:T(8,128)(2,1)} fusion(bf16[32,512,512]{2,1,0:T(8,128)(2,1)} %bitcast.34, s32[]{:T(128)S(6)} %select_n.99), kind=kLoop, calls=%fused_computation.39 | loop fusion | bytes 16777220 | tf_op jit(solution)/shard_map/dynamic_slice | solution.py:349
  138.2 24.0 %shard_map.124 = (bf16[8,512,512]{2,1,0:T(8,128)(2,1)}, f32[8,8,512]{2,1,0:T(8,128)}) custom-call(s32[3]{0:T(128)} %pad_add_fusion.1.pos_ref.refs_0_, s32[8,8,4,256]{3,2,1,0:T(4,128)} %get-tuple-element.25.refs_1_, f32[8,8,1,256]{3,2,1,0:T(1,128)} %get-tuple-element.29.refs_2_, bf16[512,512]{1,0:T(8,128)(2,1)} %bitcast.39, bf16[512,512]{1,0:T(8,128)(2,1)} %copy-done.11, ...), custom_call_target="tpu_custom_call" | custom-call | flops 17179869184 | bytes 8847372 | tf_op jit(solution)/shard_map/pallas_call | solution.py:41
  163.6 28.5 %shard_map.125 = (bf16[512,256]{1,0:T(8,128)(2,1)}, bf16[8,512,512]{2,1,0:T(8,128)(2,1)}) custom-call(s32[3]{0:T(128)} %pad_add_fusion.1.pos_ref.refs_0_, s32[8,8,4,256]{3,2,1,0:T(4,128)} %get-tuple-element.25.refs_1_, f32[8,32,256]{2,1,0:T(8,128)} %get-tuple-element.28.refs_2_, bf16[32,256,512]{2,1,0:T(8,128)(2,1)} %constant_dynamic-slice_fusion.1.refs_3_, ...), custom_call_target="tpu_custom_call" | custom-call | flops 17179869184 | bytes 17956876 | tf_op jit(solution)/shard_map/pallas_call | solution.py:41
  192.1 1.6 collective-permute-start.20
  193.7 0.8 pad_maximum_fusion
  194.5 6.8 %shard_map.126 = f32[512,512]{1,0:T(8,128)} custom-call(bf16[8,512,512]{2,1,0:T(8,128)(2,1)} %get-tuple-element.33.mix_ref, bf16[8,512,512]{2,1,0:T(8,128)(2,1)} %get-tuple-element.34.scaled_ref), custom_call_target="tpu_custom_call" | custom-call | flops 2147483648 | bytes 9437184 | tf_op jit(solution)/shard_map/pallas_call | solution.py:41
  201.4 0.8 pad_maximum_fusion.2
  (88 shorter events, 11.0 us)
Async XLA Ops:
  1.9 54.5 %copy-start.1 = (bf16[512,512]{0,1:T(8,128)(2,1)}, bf16[512,512]{0,1:T(8,128)(2,1)S(1)}, u32[]{:S(2)}) copy-start(bf16[512,512]{0,1:T(8,128)(2,1)S(1)} %copy.15) | copy-start | bytes 1572868
  1.9 19.5 %collective-permute-start.3 = (bf16[512,512]{1,0:T(8,128)(2,1)S(1)}, bf16[512,512]{1,0:T(8,128)(2,1)S(1)}, u32[]{:S(2)}, u32[]{:S(2)}) collective-permute-start(bf16[512,512]{1,0:T(8,128)(2,1)S(1)} %bitcast.35), channel_id=1, source_target_pairs={{0,4},{1,5},{2,6},{3,7},{4,0},{5,1},{6,2},{7,3},{8,12},{9,13},{10,... | collective-permute-start | bytes 1572872 | tf_op jit(solution)/shard_map/ppermute | solution.py:272
  4.9 18.4 %collective-permute-start.1 = (bf16[512,512]{1,0:T(8,128)(2,1)S(1)}, bf16[512,512]{1,0:T(8,128)(2,1)S(1)}, u32[]{:S(2)}, u32[]{:S(2)}) collective-permute-start(bf16[512,512]{1,0:T(8,128)(2,1)S(1)} %bitcast.36), channel_id=1, source_target_pairs={{0,2},{1,3},{2,0},{3,1},{4,6},{5,7},{6,4},{7,5},{8,10},{9,11},{10,... | collective-permute-start | bytes 1572872 | tf_op jit(solution)/shard_map/ppermute | solution.py:272
  17.5 39.7 %all-to-all-start = ((s32[32,4,512]{2,1,0:T(4,128)}), s32[32,4,512]{2,1,0:T(4,128)S(1)}, u32[]{:S(2)}, u32[]{:S(2)}) async-start(s32[32,4,512]{2,1,0:T(4,128)} %broadcast_in_dim.11), calls=%async_computation | async-start | bytes 524288 | tf_op jit(solution)/shard_map/all_to_all | solution.py:339
  21.4 35.0 %copy-start.6 = (bf16[512,512]{1,0:T(8,128)(2,1)}, bf16[512,512]{1,0:T(8,128)(2,1)S(1)}, u32[]{:S(2)}) copy-start(bf16[512,512]{1,0:T(8,128)(2,1)S(1)} %collective-permute-done.3.refs_10_.refs_7_) | copy-start | bytes 1572868
  21.5 11.3 %collective-permute-start.5 = (bf16[256,512]{1,0:T(8,128)(2,1)S(1)}, bf16[256,512]{1,0:T(8,128)(2,1)}, u32[]{:S(2)}, u32[]{:S(2)}) collective-permute-start(bf16[256,512]{1,0:T(8,128)(2,1)S(1)} %slice.50), channel_id=1, source_target_pairs={{0,2},{1,3},{2,0},{3,1},{4,6},{5,7},{6,4},{7,5},{8,10},{9,11},{10,... | collective-permute-start | bytes 786440 | tf_op jit(solution)/shard_map/ppermute | solution.py:272
  23.3 33.1 %copy-start.7 = (bf16[512,512]{1,0:T(8,128)(2,1)}, bf16[512,512]{1,0:T(8,128)(2,1)S(1)}, u32[]{:S(2)}) copy-start(bf16[512,512]{1,0:T(8,128)(2,1)S(1)} %collective-permute-done.1.refs_8_.refs_5_) | copy-start | bytes 1572868
  23.3 10.3 %collective-permute-start.6 = (bf16[256,512]{1,0:T(8,128)(2,1)S(1)}, bf16[256,512]{1,0:T(8,128)(2,1)}, u32[]{:S(2)}, u32[]{:S(2)}) collective-permute-start(bf16[256,512]{1,0:T(8,128)(2,1)S(1)} %slice.51), channel_id=1, source_target_pairs={{0,4},{1,5},{2,6},{3,7},{4,0},{5,1},{6,2},{7,3},{8,12},{9,13},{10,... | collective-permute-start | bytes 786440 | tf_op jit(solution)/shard_map/ppermute | solution.py:272
  24.9 49.8 %collective-permute-start = (bf16[512,512]{1,0:T(8,128)(2,1)S(1)}, bf16[512,512]{1,0:T(8,128)(2,1)S(1)}, u32[]{:S(2)}, u32[]{:S(2)}) collective-permute-start(bf16[512,512]{1,0:T(8,128)(2,1)S(1)} %bitcast.37), channel_id=1, source_target_pairs={{0,1},{1,0},{2,3},{3,2},{4,5},{5,4},{6,7},{7,6},{8,9},{9,8},{10,11... | collective-permute-start | bytes 1572872 | tf_op jit(solution)/shard_map/ppermute | solution.py:272
  24.9 49.8 %collective-permute-start.2 = (bf16[512,512]{1,0:T(8,128)(2,1)S(1)}, bf16[512,512]{1,0:T(8,128)(2,1)}, u32[]{:S(2)}, u32[]{:S(2)}) collective-permute-start(bf16[512,512]{1,0:T(8,128)(2,1)S(1)} %collective-permute-done.1.refs_8_.refs_5_), channel_id=1, source_target_pairs={{0,1},{1,0},{2,3},{3,2},{4,5},{5,4},{6,7},{7,6},{8,9},{9,8},{10,11... | collective-permute-start | bytes 1572872 | tf_op jit(solution)/shard_map/ppermute | solution.py:272
  25.4 49.3 %collective-permute-start.4 = (bf16[512,512]{1,0:T(8,128)(2,1)S(1)}, bf16[512,512]{1,0:T(8,128)(2,1)}, u32[]{:S(2)}, u32[]{:S(2)}) collective-permute-start(bf16[512,512]{1,0:T(8,128)(2,1)S(1)} %collective-permute-done.3.refs_10_.refs_7_), channel_id=1, source_target_pairs={{0,1},{1,0},{2,3},{3,2},{4,5},{5,4},{6,7},{7,6},{8,9},{9,8},{10,11... | collective-permute-start | bytes 1572872 | tf_op jit(solution)/shard_map/ppermute | solution.py:272
  32.8 41.8 %collective-permute-start.7 = (bf16[256,512]{1,0:T(8,128)(2,1)}, bf16[256,512]{1,0:T(8,128)(2,1)S(1)}, u32[]{:S(2)}, u32[]{:S(2)}) collective-permute-start(bf16[256,512]{1,0:T(8,128)(2,1)} %collective-permute-done.5.refs_12_.refs_9_), channel_id=1, source_target_pairs={{0,1},{1,0},{2,3},{3,2},{4,5},{5,4},{6,7},{7,6},{8,9},{9,8},{10,11... | collective-permute-start | bytes 786440 | tf_op jit(solution)/shard_map/ppermute | solution.py:272
  33.6 41.1 %collective-permute-start.8 = (bf16[256,512]{1,0:T(8,128)(2,1)}, bf16[256,512]{1,0:T(8,128)(2,1)S(1)}, u32[]{:S(2)}, u32[]{:S(2)}) collective-permute-start(bf16[256,512]{1,0:T(8,128)(2,1)} %collective-permute-done.6.refs_13_.refs_10_), channel_id=1, source_target_pairs={{0,1},{1,0},{2,3},{3,2},{4,5},{5,4},{6,7},{7,6},{8,9},{9,8},{10,11... | collective-permute-start | bytes 786440 | tf_op jit(solution)/shard_map/ppermute | solution.py:272
  35.9 20.5 %copy-start.10 = (f32[1000,32]{0,1:T(8,128)S(1)}, f32[1000,32]{0,1:T(8,128)}, u32[]{:S(2)}) copy-start(f32[1000,32]{0,1:T(8,128)} %param.15) | copy-start | bytes 384004
  103.3 8.9 %collective-permute-start.10 = (bf16[256,512]{1,0:T(8,128)(2,1)}, bf16[256,512]{1,0:T(8,128)(2,1)S(1)}, u32[]{:S(2)}, u32[]{:S(2)}) collective-permute-start(bf16[256,512]{1,0:T(8,128)(2,1)} %get-tuple-element.31), channel_id=1, source_target_pairs={{0,8},{8,0},{16,24},{24,16},{1,9},{9,1},{17,25},{25,17},{2,10},{10... | collective-permute-start | bytes 786440 | tf_op jit(solution)/shard_map/ppermute | solution.py:272
  113.3 23.8 %copy-start.2 = (bf16[512,512]{1,0:T(8,128)(2,1)}, bf16[512,512]{1,0:T(8,128)(2,1)S(1)}, u32[]{:S(2)}) copy-start(bf16[512,512]{1,0:T(8,128)(2,1)S(1)} %pad_maximum_fusion.1.refs_6_) | copy-start | bytes 1572868
  113.3 13.6 %collective-permute-start.14 = (bf16[512,512]{1,0:T(8,128)(2,1)S(1)}, bf16[512,512]{1,0:T(8,128)(2,1)S(1)}, u32[]{:S(2)}, u32[]{:S(2)}) collective-permute-start(bf16[512,512]{1,0:T(8,128)(2,1)S(1)} %pad_maximum_fusion.1.refs_6_), channel_id=1, source_target_pairs={{0,4},{1,5},{2,6},{3,7},{4,0},{5,1},{6,2},{7,3},{8,12},{9,13},{10,... | collective-permute-start | bytes 1572872 | tf_op jit(solution)/shard_map/ppermute | solution.py:272
  114.3 13.5 %collective-permute-start.12 = (bf16[512,512]{1,0:T(8,128)(2,1)S(1)}, bf16[512,512]{1,0:T(8,128)(2,1)S(1)}, u32[]{:S(2)}, u32[]{:S(2)}) collective-permute-start(bf16[512,512]{1,0:T(8,128)(2,1)S(1)} %pad_maximum_fusion.1.refs_6_), channel_id=1, source_target_pairs={{0,2},{1,3},{2,0},{3,1},{4,6},{5,7},{6,4},{7,5},{8,10},{9,11},{10,... | collective-permute-start | bytes 1572872 | tf_op jit(solution)/shard_map/ppermute | solution.py:272
  115.0 22.5 %collective-permute-start.9 = (bf16[512,256]{1,0:T(8,128)(2,1)}, bf16[512,256]{1,0:T(8,128)(2,1)S(1)}, u32[]{:S(2)}, u32[]{:S(2)}) collective-permute-start(bf16[512,256]{1,0:T(8,128)(2,1)} %get-tuple-element.27), channel_id=1, source_target_pairs={{0,8},{8,0},{16,24},{24,16},{1,9},{9,1},{17,25},{25,17},{2,10},{10... | collective-permute-start | bytes 786440 | tf_op jit(solution)/shard_map/ppermute | solution.py:272
  126.9 10.7 %copy-start.8 = (bf16[512,512]{1,0:T(8,128)(2,1)}, bf16[512,512]{1,0:T(8,128)(2,1)S(1)}, u32[]{:S(2)}) copy-start(bf16[512,512]{1,0:T(8,128)(2,1)S(1)} %collective-permute-done.14.refs_10_) | copy-start | bytes 1572868
  126.9 10.7 %collective-permute-start.16 = (bf16[256,512]{1,0:T(8,128)(2,1)S(1)}, bf16[256,512]{1,0:T(8,128)(2,1)S(1)}, u32[]{:S(2)}, u32[]{:S(2)}) collective-permute-start(bf16[256,512]{1,0:T(8,128)(2,1)S(1)} %slice.52), channel_id=1, source_target_pairs={{0,2},{1,3},{2,0},{3,1},{4,6},{5,7},{6,4},{7,5},{8,10},{9,11},{10,... | collective-permute-start | bytes 786440 | tf_op jit(solution)/shard_map/ppermute | solution.py:272
  127.9 10.3 %collective-permute-start.17 = (bf16[256,512]{1,0:T(8,128)(2,1)S(1)}, bf16[256,512]{1,0:T(8,128)(2,1)S(1)}, u32[]{:S(2)}, u32[]{:S(2)}) collective-permute-start(bf16[256,512]{1,0:T(8,128)(2,1)S(1)} %slice.53), channel_id=1, source_target_pairs={{0,4},{1,5},{2,6},{3,7},{4,0},{5,1},{6,2},{7,3},{8,12},{9,13},{10,... | collective-permute-start | bytes 786440 | tf_op jit(solution)/shard_map/ppermute | solution.py:272
  137.1 25.2 %collective-permute-start.11 = (bf16[512,512]{1,0:T(8,128)(2,1)S(1)}, bf16[512,512]{1,0:T(8,128)(2,1)S(1)}, u32[]{:S(2)}, u32[]{:S(2)}) collective-permute-start(bf16[512,512]{1,0:T(8,128)(2,1)S(1)} %pad_maximum_fusion.1.refs_6_), channel_id=1, source_target_pairs={{0,1},{1,0},{2,3},{3,2},{4,5},{5,4},{6,7},{7,6},{8,9},{9,8},{10,11... | collective-permute-start | bytes 1572872 | tf_op jit(solution)/shard_map/ppermute | solution.py:272
  137.1 25.3 %collective-permute-start.13 = (bf16[512,512]{1,0:T(8,128)(2,1)S(1)}, bf16[512,512]{1,0:T(8,128)(2,1)S(1)}, u32[]{:S(2)}, u32[]{:S(2)}) collective-permute-start(bf16[512,512]{1,0:T(8,128)(2,1)S(1)} %collective-permute-done.12.refs_8_), channel_id=1, source_target_pairs={{0,1},{1,0},{2,3},{3,2},{4,5},{5,4},{6,7},{7,6},{8,9},{9,8},{10,11... | collective-permute-start | bytes 1572872 | tf_op jit(solution)/shard_map/ppermute | solution.py:272
  137.6 24.8 %collective-permute-start.15 = (bf16[512,512]{1,0:T(8,128)(2,1)S(1)}, bf16[512,512]{1,0:T(8,128)(2,1)S(1)}, u32[]{:S(2)}, u32[]{:S(2)}) collective-permute-start(bf16[512,512]{1,0:T(8,128)(2,1)S(1)} %collective-permute-done.14.refs_10_), channel_id=1, source_target_pairs={{0,1},{1,0},{2,3},{3,2},{4,5},{5,4},{6,7},{7,6},{8,9},{9,8},{10,11... | collective-permute-start | bytes 1572872 | tf_op jit(solution)/shard_map/ppermute | solution.py:272
  137.7 24.6 %copy-start.17 = (bf16[256,512]{1,0:T(8,128)(2,1)}, bf16[256,512]{1,0:T(8,128)(2,1)S(1)}, u32[]{:S(2)}) copy-start(bf16[256,512]{1,0:T(8,128)(2,1)S(1)} %collective-permute-done.16.refs_12_) | copy-start | bytes 786436
  137.7 24.7 %collective-permute-start.18 = (bf16[256,512]{1,0:T(8,128)(2,1)S(1)}, bf16[256,512]{1,0:T(8,128)(2,1)S(1)}, u32[]{:S(2)}, u32[]{:S(2)}) collective-permute-start(bf16[256,512]{1,0:T(8,128)(2,1)S(1)} %collective-permute-done.16.refs_12_), channel_id=1, source_target_pairs={{0,1},{1,0},{2,3},{3,2},{4,5},{5,4},{6,7},{7,6},{8,9},{9,8},{10,11... | collective-permute-start | bytes 786440 | tf_op jit(solution)/shard_map/ppermute | solution.py:272
  138.1 24.1 %copy-start.18 = (bf16[256,512]{1,0:T(8,128)(2,1)}, bf16[256,512]{1,0:T(8,128)(2,1)S(1)}, u32[]{:S(2)}) copy-start(bf16[256,512]{1,0:T(8,128)(2,1)S(1)} %collective-permute-done.17.refs_13_) | copy-start | bytes 786436
  138.1 24.2 %collective-permute-start.19 = (bf16[256,512]{1,0:T(8,128)(2,1)S(1)}, bf16[256,512]{1,0:T(8,128)(2,1)S(1)}, u32[]{:S(2)}, u32[]{:S(2)}) collective-permute-start(bf16[256,512]{1,0:T(8,128)(2,1)S(1)} %collective-permute-done.17.refs_13_), channel_id=1, source_target_pairs={{0,1},{1,0},{2,3},{3,2},{4,5},{5,4},{6,7},{7,6},{8,9},{9,8},{10,11... | collective-permute-start | bytes 786440 | tf_op jit(solution)/shard_map/ppermute | solution.py:272
  138.2 24.1 %copy-start.4 = (bf16[512,256]{1,0:T(8,128)(2,1)S(1)}, bf16[512,256]{1,0:T(8,128)(2,1)}, u32[]{:S(2)}) copy-start(bf16[512,256]{1,0:T(8,128)(2,1)} %get-tuple-element.27) | copy-start | bytes 786436
  192.1 9.3 %copy-start.5 = (bf16[512,256]{1,0:T(8,128)(2,1)S(1)}, bf16[512,256]{1,0:T(8,128)(2,1)}, u32[]{:S(2)}) copy-start(bf16[512,256]{1,0:T(8,128)(2,1)} %get-tuple-element.32) | copy-start | bytes 786436
  192.1 9.3 %collective-permute-start.20 = (bf16[512,256]{1,0:T(8,128)(2,1)}, bf16[512,256]{1,0:T(8,128)(2,1)S(1)}, u32[]{:S(2)}, u32[]{:S(2)}) collective-permute-start(bf16[512,256]{1,0:T(8,128)(2,1)} %get-tuple-element.32), channel_id=1, source_target_pairs={{0,8},{8,0},{16,24},{24,16},{1,9},{9,1},{17,25},{25,17},{2,10},{10... | collective-permute-start | bytes 786440 | tf_op jit(solution)/shard_map/ppermute | solution.py:272
  (11 other events, 25.9 us)

commit v2 on v0

v2 whole, which is shorter than its diff:
```python
import functools

import jax
import jax.numpy as jnp
from jax import lax
from jax.experimental import pallas as pl
from jax.experimental.pallas import tpu as pltpu
from jax.sharding import PartitionSpec as P

BF = jnp.bfloat16
F32 = jnp.float32
VMEM = pl.BlockSpec(memory_space=pltpu.VMEM)
SMEM = pl.BlockSpec(memory_space=pltpu.SMEM)
ANY = pl.BlockSpec(memory_space=pl.ANY)
VMEM_LIMIT = 56 * 1024 * 1024
SPLIT = 2
TILE = 256
GATHER, SCATTER = 32, 33


def dot(a, b):
    return jnp.dot(a, b, preferred_element_type=F32)


def dot_nt(a, b):
    return lax.dot_general(a, b, (((1,), (1,)), ((), ())), preferred_element_type=F32)


def dot_tn(a, b):
    return lax.dot_general(a, b, (((0,), (0,)), ((), ())), preferred_element_type=F32)


def one_hot(row, count):
    places = lax.broadcasted_iota(jnp.int32, (count, row.shape[1]), 0)
    return jnp.where(places == row, 1.0, 0.0).astype(BF)


def one_hot_rows(column, count):
    places = lax.broadcasted_iota(jnp.int32, (column.shape[0], count), 1)
    return jnp.where(places == column, 1.0, 0.0).astype(BF)


def split3(x):
    high = x.astype(BF)
    rest = x - high.astype(F32)
    middle = rest.astype(BF)
    return high, middle, (rest - middle.astype(F32)).astype(BF)


def shape(dims, kind):
    return jax.ShapeDtypeStruct(dims, kind)


def call(kernel, outs, out_specs, ins, *args, scratch=(), flops=0):
    size = sum(a.size * a.dtype.itemsize for a in args) + sum(o.size * o.dtype.itemsize for o in outs)
    return pl.pallas_call(
        kernel,
        out_shape=tuple(outs),
        in_specs=ins,
        out_specs=tuple(out_specs),
        scratch_shapes=scratch,
        compiler_params=pltpu.CompilerParams(vmem_limit_bytes=VMEM_LIMIT),
        cost_estimate=pl.CostEstimate(flops=flops, bytes_accessed=size, transcendentals=0),
    )(*args)


def pack_kernel(counts_ref, rel_ref, src_ref, dst_ref, group_ref, out_ref, *, ents, n_ent):
    slots = rel_ref.shape[1]
    cap = slots // n_ent
    ent = lax.axis_index("ent")
    lane = lax.broadcasted_iota(jnp.int32, (1, slots), 1)
    block = lane // cap
    limit = jnp.zeros((1, slots), jnp.int32)
    last = jnp.zeros((1, slots), jnp.int32)
    for k in range(n_ent):
        limit = jnp.where(block == k, counts_ref[0, 0, k], limit)
        last = jnp.where(lane == k, counts_ref[0, 0, k], last)
    live = lane - block * cap < limit
    group = group_ref[...]
    digits = jnp.concatenate([group // 128, group % 128, jnp.zeros((14, group.shape[1]), jnp.int32)], axis=0)
    got = dot(digits.astype(F32).astype(BF), one_hot(rel_ref[...], group.shape[1])).astype(jnp.int32)
    packed = jnp.concatenate([
        got[0:1] * 128 + got[1:2],
        src_ref[...] - ent * ents,
        jnp.where(live, dst_ref[...] - block * ents, -1),
        last,
    ], axis=0)

    def put(i, carry):
        out_ref[i] = packed
        return carry

    lax.fori_loop(0, out_ref.shape[0], put, 0)


def table_kernel(pos_ref, coeffs_ref, pieces_ref, own_ref):
    basis_count = coeffs_ref.shape[0]
    n_high = coeffs_ref.shape[1] // 128
    values = coeffs_ref[...]
    mine = coeffs_ref[pl.ds(pos_ref[0], 1), :]
    n = n_high * basis_count
    for h in range(n_high):
        for i, piece in enumerate(split3(values[:, h * 128:(h + 1) * 128])):
            pieces_ref[i * n + h * basis_count:i * n + (h + 1) * basis_count, :] = piece
    own = [mine[:, h * 128:(h + 1) * 128] for h in range(n_high)]
    own.append(jnp.zeros((own_ref.shape[0] // 3 - n_high, 128), F32))
    own_ref[...] = jnp.concatenate(split3(jnp.concatenate(own, axis=0)), axis=0)


def coefficients(pieces, rel_row, basis_count, n_high):
    high = rel_row // 128
    got = dot(pieces, one_hot(rel_row % 128, 128))
    n = n_high * basis_count
    got = got[:n] + got[n:2 * n] + got[2 * n:]
    total = jnp.zeros((basis_count, rel_row.shape[1]), F32)
    for i in range(n_high):
        total += jnp.where(high == i, got[i * basis_count:(i + 1) * basis_count], 0.0)
    return total


def slot_rows(coef, gather, scatter):
    basis_count, lanes = coef.shape
    wide = -(-lanes // 128) * 128
    rows = jnp.concatenate(
        [coef, gather.astype(F32), scatter.astype(F32), jnp.zeros((128 - basis_count - 2, lanes), F32)], axis=0
    )
    if wide != lanes:
        rows = jnp.concatenate([rows, jnp.zeros((128, wide - lanes), F32)], axis=1)
    return rows.T[:lanes]


def clear_rows(ref):
    lane = lax.broadcasted_iota(jnp.int32, ref.shape, 1)
    ref[...] = jnp.where((lane == GATHER) | (lane == SCATTER), -1.0, 0.0)


def put_blocks(ref, rows, at, cap, counts):
    for g, count in enumerate(counts):
        ref[pl.ds(pl.multiple_of(at, 8), cap), :] = rows[g * cap:(g + 1) * cap]
        at = at + (count + 7) // 8 * 8
    return at


def prep_in_kernel(counts_ref, meta_ref, pieces_ref, rows_ref, ends_ref, *, n_rel, n_ent, ents, count):
    ent = lax.axis_index("ent")
    slots = meta_ref.shape[2]
    cap = slots // n_ent
    n_high = pieces_ref.shape[0] // (3 * count)
    clear_rows(rows_ref)

    def sender(m, at):
        s = ent ^ m
        ends_ref[m] = at
        block = jnp.concatenate(
            [pltpu.roll(meta_ref[g * n_ent + s], slots - ent * cap, 1)[:, :cap] for g in range(n_rel)], axis=1
        )
        coef = coefficients(pieces_ref[...], block[0:1, :], count, n_high)
        rows = slot_rows(coef, block[1:2, :] + m * ents, block[2:3, :])
        return put_blocks(rows_ref, rows, at, cap, [counts_ref[g * n_ent + s, ent] for g in range(n_rel)])

    ends_ref[n_ent] = lax.fori_loop(0, n_ent, sender, jnp.int32(0), unroll=n_ent <= 8)


def prep_rest_kernel(counts_ref, meta_ref, pieces_ref, own_ref, slots_ref, coef_b_ref, rows_ref, ends_ref,
                     *, n_rel, n_ent, ents, count):
    ent = lax.axis_index("ent")
    cap = meta_ref.shape[2] // n_ent
    lanes = n_rel * cap
    n_high = pieces_ref.shape[0] // (3 * count)
    n_own = own_ref.shape[0] // 3
    clear_rows(rows_ref)

    def regroup(s, carry):
        for g in range(n_rel):
            block = meta_ref[g * n_ent + s]
            for k in range(n_ent):
                slots_ref[s, k, :, g * cap:(g + 1) * cap] = block[:, k * cap:(k + 1) * cap]
        return carry

    lax.fori_loop(0, n_ent, regroup, 0)

    def receiver(n, at):
        k = ent ^ n
        ends_ref[n] = at
        block = slots_ref[ent, k]
        coef = coefficients(pieces_ref[...], block[0:1, :], count, n_high)
        live = block[2:3, :] >= 0
        rows = slot_rows(coef, jnp.where(live, block[2:3, :] + n * ents, -1), jnp.where(live, block[1:2, :], -1))
        return put_blocks(rows_ref, rows, at, cap, [counts_ref[g * n_ent + ent, k] for g in range(n_rel)])

    ends_ref[n_ent] = lax.fori_loop(0, n_ent, receiver, jnp.int32(0), unroll=n_ent <= 8)

    def sender(s, carry):
        rel = jnp.concatenate([slots_ref[s, k, 0:1, :] for k in range(n_ent)], axis=1)
        got = dot(own_ref[...], one_hot(rel % 128, 128))
        got = got[:n_own] + got[n_own:2 * n_own] + got[2 * n_own:]
        mine = lax.broadcasted_iota(jnp.int32, got.shape, 0) == rel // 128
        picked = jnp.sum(jnp.where(mine, got, 0.0), axis=0, keepdims=True)
        for k in range(n_ent):
            coef_b_ref[s, k] = picked[:, k * lanes:(k + 1) * lanes]
        return carry

    lax.fori_loop(0, n_ent, sender, 0, unroll=n_ent <= 8)


def chunk_copies(refs, places, out_ref, sems):
    copies = []
    for i, (ref, place) in enumerate(zip(refs, places, strict=True)):
        if place is None:
            target = out_ref
        else:
            target = out_ref.at[place[0], pl.ds(place[1], ref.shape[0])]
        copies.append(pltpu.make_async_copy(ref, target, sems.at[i]))
    return copies


def gather_rows(rows_ref, ends_ref, pick, out_ref, lanes, ents, n_ent):
    last = pl.multiple_of((tiles_of(ends_ref[n_ent]) - 1) * TILE, TILE)
    out_ref[pl.ds(last, TILE), :] = jnp.zeros((TILE, out_ref.shape[1]), F32)

    def chunk(m, carry):
        at = pl.multiple_of(ends_ref[m], 8)
        column = rows_ref[pl.ds(at, lanes), GATHER:GATHER + 1].astype(jnp.int32)
        pick(m, one_hot_rows(column - m * ents, ents), pl.ds(at, lanes))
        return carry

    lax.fori_loop(0, n_ent, chunk, 0, unroll=n_ent <= 8)


def apply_bases(picked, weight, rows_ref, start, count):
    total = None
    for b in range(count):
        part = weight(b, picked) * rows_ref[pl.ds(start, TILE), b:b + 1]
        total = part if total is None else total + part
    return total


def tiles_of(end):
    return (end + TILE - 1) // TILE


def forward_kernel(*refs, places, n_ent, count):
    n_parts = len(places)
    ends_ref, rows_ref, basis_ref, wself_ref, cot_ref = refs[:5]
    chunk_refs = refs[5:5 + n_parts]
    out_ref, grad_ref, scaled_ref = refs[5 + n_parts:8 + n_parts]
    feat_ref, weights_ref, x_ref, sums_ref, sems, weight_sems = refs[8 + n_parts:]
    cols = weights_ref.shape[2]
    ents = feat_ref.shape[1]
    half = lax.axis_index("rel") % SPLIT
    loads = chunk_copies(chunk_refs, places, feat_ref, sems)
    for c in loads:
        c.start()
    weights = [
        pltpu.make_async_copy(
            basis_ref.at[b, :, pl.ds(pl.multiple_of(half * cols, cols), cols)], weights_ref.at[b], weight_sems.at[b]
        )
        for b in range(count)
    ]
    sums_ref[...] = jnp.zeros_like(sums_ref)
    for c in loads:
        c.wait()
    for c in weights:
        c.start()

    def pick(m, hot, place):
        x_ref[place, :] = dot(hot, feat_ref[m])

    gather_rows(rows_ref, ends_ref, pick, x_ref, x_ref.shape[0] // n_ent, ents, n_ent)
    for c in weights:
        c.wait()

    def tile(t, carry):
        start = pl.multiple_of(t * TILE, TILE)
        picked = x_ref[pl.ds(start, TILE), :].astype(BF)

        def weight(b, value):
            return dot(value, weights_ref[b])

        sent = apply_bases(picked, weight, rows_ref, start, count).astype(BF)
        hot = one_hot_rows(rows_ref[pl.ds(start, TILE), SCATTER:SCATTER + 1].astype(jnp.int32), ents)
        sums_ref[...] += dot_tn(hot, jnp.concatenate([sent, jnp.ones((TILE, 128), BF)], axis=1))
        return carry

    lax.fori_loop(0, tiles_of(ends_ref[n_ent]), tile, 0)
    inverse = 1.0 / jnp.maximum(sums_ref[:, cols:cols + 1], 1.0)
    pre = dot(feat_ref[0], wself_ref[...]) + sums_ref[:, :cols] * inverse
    sig = jax.nn.sigmoid(pre)
    out_ref[...] = (pre * sig).astype(BF)
    grad = (cot_ref[...].astype(F32) * (sig * (1.0 + pre * (1.0 - sig)))).astype(BF)
    grad_ref[...] = grad
    scaled_ref[...] = (grad.astype(F32) * inverse).astype(BF)


def mix_kernel(*refs, places, n_ent, rows, chunks):
    n_parts = len(places)
    pos_ref, slots_ref, coef_ref = refs[:3]
    chunk_refs = refs[3:3 + n_parts]
    mix_out_ref = refs[3 + n_parts]
    feat_ref, mix_ref, hot_ref, sems = refs[4 + n_parts:]
    ent = lax.axis_index("ent")
    ents = feat_ref.shape[1]
    lanes = slots_ref.shape[3]
    loads = chunk_copies(chunk_refs, places, feat_ref, sems)
    for c in loads:
        c.start()
    for c in loads:
        c.wait()
    first = pl.multiple_of(pos_ref[1], 128)

    def receiver(i, carry):
        k = ent ^ (chunks[0] + i)
        for m in range(n_ent):
            s = ent ^ m
            at = slice(m * lanes, (m + 1) * lanes)
            got = dot_tn(feat_ref[m, :, pl.ds(first, rows)], one_hot(slots_ref[s, k, 1:2, :], ents))
            mix_ref[:, at] = (got * coef_ref[s, k]).astype(BF)
            hot_ref[:, at] = one_hot(slots_ref[s, k, 2:3, :], ents)
        mix_out_ref[i] = dot_nt(mix_ref[...], hot_ref[...]).astype(BF)
        return carry

    lax.fori_loop(0, chunks[1] - chunks[0], receiver, 0)


def backward_kernel(*refs, places, n_ent, count):
    n_parts = len(places)
    ends_ref, rows_ref, basis_ref, wself_ref, pre_ref, other_ref = refs[:6]
    chunk_refs = refs[6:6 + 2 * n_parts]
    out_ref = refs[6 + 2 * n_parts]
    grad_ref, weights_ref, h_ref, sums_ref, sems, weight_sems = refs[7 + 2 * n_parts:]
    cols = weights_ref.shape[1]
    ents = grad_ref.shape[2]
    half = lax.axis_index("rel") % SPLIT
    own_at = pl.multiple_of(half * cols, cols)
    other_at = pl.multiple_of((1 - half) * cols, cols)
    loads = chunk_copies(chunk_refs[:n_parts], places, grad_ref.at[0], sems.at[0])
    loads += chunk_copies(chunk_refs[n_parts:], places, grad_ref.at[1], sems.at[1])
    for c in loads:
        c.start()
    weights = [
        pltpu.make_async_copy(basis_ref.at[b, pl.ds(own_at, cols)], weights_ref.at[b], weight_sems.at[b])
        for b in range(count)
    ]
    sums_ref[...] = jnp.zeros_like(sums_ref)
    for c in loads:
        c.wait()
    for c in weights:
        c.start()

    def pick(n, hot, place):
        h_ref[place, pl.ds(own_at, cols)] = dot(hot, grad_ref[0, n])
        h_ref[place, pl.ds(other_at, cols)] = dot(hot, grad_ref[1, n])

    gather_rows(rows_ref, ends_ref, pick, h_ref, h_ref.shape[0] // n_ent, ents, n_ent)
    for c in weights:
        c.wait()

    def tile(t, carry):
        start = pl.multiple_of(t * TILE, TILE)
        picked = h_ref[pl.ds(start, TILE), :].astype(BF)

        def weight(b, value):
            return dot_nt(value, weights_ref[b])

        total = apply_bases(picked, weight, rows_ref, start, count)
        high = total.astype(BF)
        low = (total - high.astype(F32)).astype(BF)
        hot = one_hot_rows(rows_ref[pl.ds(start, TILE), SCATTER:SCATTER + 1].astype(jnp.int32), ents)
        sums_ref[...] += dot_tn(hot, high) + dot_tn(hot, low)
        return carry

    lax.fori_loop(0, tiles_of(ends_ref[n_ent]), tile, 0)
    self_part = dot_nt(pre_ref[...], wself_ref[:, pl.ds(own_at, cols)])
    self_part += dot_nt(other_ref[...], wself_ref[:, pl.ds(other_at, cols)])
    out_ref[...] = (self_part + sums_ref[...]).astype(BF)


def basis_kernel(*refs, places, n_mix):
    n_parts = len(places)
    mix_refs = refs[:n_mix]
    chunk_refs = refs[n_mix:n_mix + 2 * n_parts]
    out_ref = refs[n_mix + 2 * n_parts]
    grad_ref, sems = refs[n_mix + 2 * n_parts + 1:]
    cols = grad_ref.shape[3]
    half = lax.axis_index("rel") % SPLIT
    loads = chunk_copies(chunk_refs[:n_parts], places, grad_ref.at[0], sems.at[0])
    loads += chunk_copies(chunk_refs[n_parts:], places, grad_ref.at[1], sems.at[1])
    for c in loads:
        c.start()
    for c in loads:
        c.wait()
    for side in range(SPLIT):
        total, n = None, 0
        for mix in mix_refs:
            for i in range(mix.shape[0]):
                part = dot(mix[i], grad_ref[side, n])
                total = part if total is None else total + part
                n += 1
        at = (half if side == 0 else 1 - half) * cols
        out_ref[:, pl.ds(pl.multiple_of(at, cols), cols)] = total


def exchange(x, mask, axis):
    count = lax.axis_size(axis)
    return lax.ppermute(x, axis, [(i, i ^ mask) for i in range(count)])


def stacked(x):
    n_ent = lax.axis_size("ent")
    whole = lax.all_gather(x, "ent", axis=0)
    return whole[lax.axis_index("ent") ^ jnp.arange(n_ent, dtype=jnp.int32)]


def feature_chunks(x, first, second):
    if lax.axis_size("ent") != 8:
        return [second(first([stacked(x)]))[0]], [None]
    rows = x.shape[0] // 2
    a, b = first([exchange(x, 2, "ent"), exchange(x, 4, "ent")])
    c = exchange(x, 1, "ent")
    top, low = second([exchange(b[:rows], 2, "ent"), exchange(a[rows:], 4, "ent")])
    parts = [x, c, a, exchange(a, 1, "ent"), b, exchange(b, 1, "ent")]
    parts += [top, low, exchange(top, 1, "ent"), exchange(low, 1, "ent")]
    return parts, [(m, 0) for m in range(6)] + [(6, 0), (6, rows), (7, 0), (7, rows)]


def half_chunks(own, other_of, first, second, third):
    if lax.axis_size("ent") != 8:
        (other,) = first([other_of()])
        other = third(second([other]))[0]
        return [stacked(own)], [stacked(other)], [None]
    a0, b0, c0 = exchange(own, 2, "ent"), exchange(own, 4, "ent"), exchange(own, 1, "ent")
    other, a0, b0 = first([other_of(), a0, b0])
    a1, b1, c1 = exchange(other, 2, "ent"), exchange(other, 4, "ent"), exchange(other, 1, "ent")
    d0 = exchange(b0, 2, "ent")
    ca0, cb0 = exchange(a0, 1, "ent"), exchange(b0, 1, "ent")
    a1, b1, d0 = second([a1, b1, d0])
    d1 = exchange(a1, 4, "ent")
    ca1, cb1, cd0 = exchange(a1, 1, "ent"), exchange(b1, 1, "ent"), exchange(d0, 1, "ent")
    (d1,) = third([d1])
    return (
        [own, c0, a0, ca0, b0, cb0, d0, cd0],
        [other, c1, a1, ca1, b1, cb1, d1, exchange(d1, 1, "ent")],
        [(m, 0) for m in range(8)],
    )


def join(own, other, half):
    swap = half == 1
    return jnp.concatenate([jnp.where(swap, other, own), jnp.where(swap, own, other)], axis=1)


def per_device(features, w_self, basis_mats, basis_coeffs, group_rels, rel_local, edge_src,
               edge_dst, block_counts, cotangent):
    ents, depth = features.shape
    n_ent, n_rel = lax.axis_size("ent"), lax.axis_size("rel")
    slots = rel_local.shape[0]
    cap = slots // n_ent
    lanes = n_rel * cap
    n_rels, count = basis_coeffs.shape
    n_dev = n_rel * n_ent
    rows = count * depth // n_dev
    cols = depth // SPLIT
    rel = lax.axis_index("rel")
    half = rel % SPLIT
    all_lanes = n_ent * lanes

    (meta,) = call(
        functools.partial(pack_kernel, ents=ents, n_ent=n_ent),
        [shape((n_dev, 4, slots), jnp.int32)], [VMEM], [SMEM] + [VMEM] * 4,
        block_counts, rel_local[None], edge_src[None], edge_dst[None],
        group_rels[None],
    )
    meta = lax.all_to_all(meta, ("rel", "ent"), 0, 0, tiled=True)
    counts = meta[:, 3, :n_ent]

    first_row = (rel * n_ent + lax.axis_index("ent")) * rows
    pos = jnp.stack([first_row // depth, first_row % depth]).astype(jnp.int32)
    basis = basis_mats.reshape(count, depth, depth)
    wself_cols = lax.dynamic_slice_in_dim(w_self, half * cols, cols, axis=1)
    wself_rows = lax.dynamic_slice_in_dim(w_self, half * cols, cols, axis=0)
    cot = lax.dynamic_slice_in_dim(cotangent, half * cols, cols, axis=1)
    padded = -(-n_rels // 128) * 128
    coeffs_t = jnp.pad(basis_coeffs, ((0, padded - n_rels), (0, 0))).T

    n_high = padded // 128
    n_own = -(-(n_high + 1) // 16) * 16
    pieces, own_pieces = call(
        table_kernel,
        [shape((3 * n_high * count, 128), BF), shape((3 * n_own, 128), BF)],
        [VMEM, VMEM], [SMEM, VMEM], pos, coeffs_t,
    )
    row_shape = shape((all_lanes, 128), F32)
    ends_shape = shape((n_ent + 1,), jnp.int32)
    inputs = [pieces, own_pieces, wself_cols, cot]

    def beside_first(arrived):
        tied = lax.optimization_barrier((*arrived, *inputs))
        inputs[:] = tied[len(arrived):]
        return tied[:len(arrived)]

    def beside_second(arrived):
        pieces = inputs[0]
        made = call(
            functools.partial(prep_in_kernel, n_rel=n_rel, n_ent=n_ent, ents=ents, count=count),
            [row_shape, ends_shape], [VMEM, SMEM], [SMEM, VMEM, VMEM],
            counts, meta, pieces,
            flops=10**9,
        )
        tied = lax.optimization_barrier((*arrived, *made))
        inputs.extend(tied[len(arrived):])
        return tied[:len(arrived)]

    feats, feat_places = feature_chunks(features, beside_first, beside_second)
    pieces, own_pieces, wself_cols, cot, rows_in, ends_in = inputs
    part_sems = pltpu.SemaphoreType.DMA((len(feats),))
    out_cols, pre_cols, scaled_cols = call(
        functools.partial(forward_kernel, places=feat_places, n_ent=n_ent, count=count),
        [shape((ents, cols), BF)] * 3, [VMEM] * 3,
        [SMEM, VMEM, ANY, VMEM, VMEM] + [ANY] * len(feats),
        ends_in, rows_in, basis, wself_cols, cot, *feats,
        scratch=[
            pltpu.VMEM((n_ent, ents, depth), BF),
            pltpu.VMEM((count, depth, cols), BF),
            pltpu.VMEM((all_lanes, depth), F32),
            pltpu.VMEM((ents, cols + 128), F32),
            part_sems,
            pltpu.SemaphoreType.DMA((count,)),
        ],
        flops=2 * all_lanes * count * depth * cols,
    )
    other_pre = []
    made = []

    def tie(arrived, *others):
        tied = lax.optimization_barrier((*arrived, *others))
        made.extend(tied[len(arrived):])
        return tied[:len(arrived)]

    def prep_rest(arrived):
        return tie(arrived, *call(
            functools.partial(prep_rest_kernel, n_rel=n_rel, n_ent=n_ent, ents=ents, count=count),
            [shape((n_ent, n_ent, 4, lanes), jnp.int32), shape((n_ent, n_ent, 1, lanes), F32), row_shape, ends_shape],
            [VMEM, VMEM, VMEM, SMEM], [SMEM, VMEM, VMEM, VMEM],
            counts, meta, pieces, own_pieces,
            flops=10**9,
        ))

    def mix(arrived, low, high):
        grouped, coef_b = made[:2]
        return tie(arrived, *call(
            functools.partial(mix_kernel, places=feat_places, n_ent=n_ent, rows=rows, chunks=(low, high)),
            [shape((high - low, rows, ents), BF)], [VMEM],
            [SMEM, VMEM, VMEM] + [ANY] * len(feats),
            pos, grouped, coef_b, *feats,
            scratch=[
                pltpu.VMEM((n_ent, ents, depth), BF),
                pltpu.VMEM((rows, all_lanes), BF),
                pltpu.VMEM((ents, all_lanes), BF),
                part_sems,
            ],
            flops=4 * (high - low) * n_ent * lanes * rows * ents,
        ))

    def mix_first(arrived):
        other_pre.append(exchange(pre_cols, 1, "rel"))
        return mix(arrived, 0, n_ent // 2)

    own_parts, other_parts, places = half_chunks(
        scaled_cols, lambda: exchange(scaled_cols, 1, "rel"), prep_rest, mix_first,
        lambda arrived: mix(arrived, n_ent // 2, n_ent),
    )
    rows_out, ends_out = made[2:4]
    mixes = made[4:]
    (other_pre,) = other_pre

    grad_scratch = pltpu.VMEM((SPLIT, n_ent, ents, cols), BF)
    grad_sems = pltpu.SemaphoreType.DMA((SPLIT, len(own_parts)))
    (grad_cols,) = call(
        functools.partial(backward_kernel, places=places, n_ent=n_ent, count=count),
        [shape((ents, cols), BF)], [VMEM],
        [SMEM, VMEM, ANY, VMEM, VMEM, VMEM] + [ANY] * (2 * len(own_parts)),
        ends_out, rows_out, basis, wself_rows, pre_cols, other_pre, *own_parts, *other_parts,
        scratch=[
            grad_scratch,
            pltpu.VMEM((count, cols, depth), BF),
            pltpu.VMEM((all_lanes, depth), F32),
            pltpu.VMEM((ents, cols), F32),
            grad_sems,
            pltpu.SemaphoreType.DMA((count,)),
        ],
        flops=2 * all_lanes * count * depth * cols,
    )
    grad_features = join(grad_cols, exchange(grad_cols, 1, "rel"), half)
    activations = join(out_cols, exchange(out_cols, 1, "rel"), half)
    (grad_basis,) = call(
        functools.partial(basis_kernel, places=places, n_mix=len(mixes)),
        [shape((rows, depth), F32)], [VMEM],
        [VMEM] * len(mixes) + [ANY] * (2 * len(own_parts)),
        *mixes, *own_parts, *other_parts,
        scratch=[grad_scratch, grad_sems],
        flops=2 * n_ent * rows * ents * depth,
    )
    return activations, grad_features, grad_basis


def solution(mesh):
    placed = (
        P("ent", None),
        P(),
        P(),
        P(),
        P("rel"),
        P(("rel", "ent")),
        P(("rel", "ent")),
        P(("rel", "ent")),
        P("rel", "ent", None),
        P("ent", None),
    )
    return jax.shard_map(
        per_device,
        mesh=mesh,
        in_specs=placed,
        out_specs=(P("ent", None), P("ent", None), P(("rel", "ent"), None)),
        check_vma=False,
    )
```

time: 598 us -> 146 us (0.24)
  waiting for transfers between devices: 429 us -> 9.02 us
  Pallas kernels: 0 us -> 100 us
  matrix products: 59 us -> 0 us
  local copies, waits for them, and re-layouts: 35.3 us -> 7.25 us
  blocking collectives: 25.3 us -> 0 us
  other arithmetic: 19.8 us -> 3.41 us
  starting transfers between devices: 9.71 us -> 24.7 us
  between operations: 13.9 us -> 1.09 us
    reduce_scatter x1 -> x0, waiting for transfers between devices: 354 us -> none  [per_device(): lax.psum_scatter(lax.dot_general(mixed_rows, returned, (((0,), (0,)), (()...]
    pallas_call x0 -> x9, Pallas kernels: none -> 100 us  [call(): pl.pallas_call(kernel, out_shape=tuple(outs), in_specs=ins, out_specs=tup...]
    psum x2 -> x0, waiting for transfers between devices: 66.6 us -> none  [the longest x1 38.9 us: per_device(): partial_sums, in_degree = lax.psum((partial_sums, in_degree), 'rel')]
    dot_general x6 -> x0, matrix products: 59 us -> none  [the longest x1 21.5 us: per_device(): lax.dot_general(mixed_rows, returned, (((0,), (0,)), ((), ())), preferred...]
    convert_element_type x1 -> x0, local copies, waits for them, and re-layouts: 22.5 us -> none  [per_device(): mixed_rows = (rel_coef[:, :, None] * src_rows[:, None, :]).reshape(slot_c...]
    ppermute x0 -> x27, starting transfers between devices: none -> 20.8 us  [exchange(): return lax.ppermute(x, axis, [(i, i ^ mask) for i in range(count)])]
    all_to_all x1 -> x0, blocking collectives: 13.2 us -> none  [per_device(): lax.all_to_all(grad_back.reshape(ent_count, block_cap, feat_width), 'ent'...]
    psum x1 -> x0, blocking collectives: 12.1 us -> none  [per_device(): partial_sums, in_degree = lax.psum((partial_sums, in_degree), 'rel')]
  transfers between devices with their start and end apart: 5 -> 28, of which waited for: 4 -> 7; matrix products, arithmetic and copies ran while one was open for 14% -> 5% of each run, Pallas kernels for 0% -> 34%
where the time goes in v2:
time: 146 us; the launch traced here: 145 us
  Pallas kernels  100 us (68%)
  starting transfers between devices  24.7 us (17%)
  waiting for transfers between devices  9.02 us (6%)
  local copies, waits for them, and re-layouts  7.25 us (5%)
  other arithmetic  3.41 us (2%)
    pallas_call x9, Pallas kernels, call(): pl.pallas_call(kernel, out_shape=tuple(outs), in_specs=ins, out_specs=tup...  100 us
    ppermute x27, starting transfers between devices, exchange(): return lax.ppermute(x, axis, [(i, i ^ mask) for i in range(count)])  20.8 us
    ppermute x27, waiting for transfers between devices, exchange(): return lax.ppermute(x, axis, [(i, i ^ mask) for i in range(count)])  9.02 us
    all_to_all x1, starting transfers between devices, per_device(): meta = lax.all_to_all(meta, ('rel', 'ent'), 0, 0, tiled=True)  3.97 us
  transfers between devices with their start and end apart: 28, of which 7 were waited for; matrix products, arithmetic and copies ran while one was open for 5% of the time, Pallas kernels for 34%

profile of v2, /device:TPU:0, one launch (start us, length us, event | category | flops | bytes accessed | tf_op | source)
XLA Modules:
  0.0 145.5 jit_solution(13228148505587937763)
XLA Ops:
  0.6 3.0 %collective-permute-start = (bf16[512,512]{1,0:T(8,128)(2,1)}, bf16[512,512]{1,0:T(8,128)(2,1)S(1)}, u32[]{:S(2)}, u32[]{:S(2)}) collective-permute-start(bf16[512,512]{1,0:T(8,128)(2,1)} %refs_3_.3), channel_id=1, source_target_pairs={{0,2},{1,3},{2,0},{3,1},{4,6},{5,7},{6,4},{7,5},{8,10},{9,11},{10,... | collective-permute-start | bytes 1572872 | tf_op jit(solution)/shard_map/ppermute | solution.py:405
  3.6 1.5 %collective-permute-start.1 = (bf16[512,512]{1,0:T(8,128)(2,1)}, bf16[512,512]{1,0:T(8,128)(2,1)S(1)}, u32[]{:S(2)}, u32[]{:S(2)}) collective-permute-start(bf16[512,512]{1,0:T(8,128)(2,1)} %refs_3_.3), channel_id=1, source_target_pairs={{0,4},{1,5},{2,6},{3,7},{4,0},{5,1},{6,2},{7,3},{8,12},{9,13},{10,... | collective-permute-start | bytes 1572872 | tf_op jit(solution)/shard_map/ppermute | solution.py:405
  5.2 1.8 %shard_map.122 = s32[32,4,512]{2,1,0:T(4,128)} custom-call(s32[1,1,8]{2,1,0:T(1,128)} %counts_ref.1, s32[1,512]{1,0:T(1,128)} %bitcast.12, s32[1,512]{1,0:T(1,128)} %bitcast.13, s32[1,512]{1,0:T(1,128)} %bitcast.14, s32[1,250]{1,0:T(1,128)} %bitcast.15), custom_call_target="tpu_custom_call" | custom-call | bytes 269320 | tf_op jit(solution)/shard_map/pallas_call | solution.py:56
  7.0 4.0 %all-to-all-start = ((s32[32,4,512]{2,1,0:T(4,128)}), s32[32,4,512]{2,1,0:T(4,128)S(1)}, u32[]{:S(2)}, u32[]{:S(2)}) async-start(s32[32,4,512]{2,1,0:T(4,128)} %shard_map.122), calls=%async_computation | async-start | bytes 524288 | tf_op jit(solution)/shard_map/all_to_all | solution.py:473
  11.7 1.6 %pad_bitcast_fusion.coeffs_ref = f32[32,1024]{1,0:T(8,128)} fusion(f32[1000,32]{0,1:T(8,128)} %param.13), kind=kLoop, calls=%fused_computation.6 | loop fusion | bytes 259072 | tf_op jit(solution)/shard_map/transpose | solution.py:483
  13.2 1.6 %shard_map.121 = (bf16[768,128]{1,0:T(8,128)(2,1)}, bf16[48,128]{1,0:T(8,128)(2,1)}) custom-call(s32[2]{0:T(128)} %pad_add_fusion.pos_ref.refs_0_, f32[32,1024]{1,0:T(8,128)} %pad_bitcast_fusion.coeffs_ref), custom_call_target="tpu_custom_call" | custom-call | bytes 339976 | tf_op jit(solution)/shard_map/pallas_call | solution.py:56
  14.9 1.9 %constant_dynamic-slice_fusion.1 = (bf16[512,256]{1,0:T(8,128)(2,1)}, bf16[512,256]{1,0:T(8,128)(2,1)}) fusion(bf16[512,512]{1,0:T(8,128)(2,1)} %param.19, s32[]{:T(128)S(6)} %select_n.44, bf16[512,512]{1,0:T(8,128)(2,1)} %param.11), kind=kLoop, calls=%fused_computation.8 | loop fusion | bytes 1048580 | tf_op jit(solution)/shard_map/dynamic_slice | solution.py:481
  16.8 0.7 collective-permute-done.refs_7_.refs_5_
  17.5 1.8 %collective-permute-done.1.refs_9_.refs_7_ = bf16[512,512]{1,0:T(8,128)(2,1)S(1)} collective-permute-done((bf16[512,512]{1,0:T(8,128)(2,1)}, bf16[512,512]{1,0:T(8,128)(2,1)S(1)}, u32[]{:S(2)}, u32[]{:S(2)}) %collective-permute-start.1) | collective-permute-done | bytes 524320 | tf_op jit(solution)/shard_map/ppermute | solution.py:405
  19.4 2.1 %collective-permute-start.3 = (bf16[256,512]{1,0:T(8,128)(2,1)S(1)}, bf16[256,512]{1,0:T(8,128)(2,1)S(1)}, u32[]{:S(2)}, u32[]{:S(2)}) collective-permute-start(bf16[256,512]{1,0:T(8,128)(2,1)S(1)} %slice.10), channel_id=1, source_target_pairs={{0,4},{1,5},{2,6},{3,7},{4,0},{5,1},{6,2},{7,3},{8,12},{9,13},{10,... | collective-permute-start | bytes 786440 | tf_op jit(solution)/shard_map/ppermute | solution.py:405
  22.8 3.3 %shard_map.123 = (f32[2048,128]{1,0:T(8,128)}, s32[9]{0:T(128)}) custom-call(s32[32,8]{1,0:T(8,128)} %bitcast.10, s32[32,4,512]{2,1,0:T(4,128)} %copy-done.1, bf16[768,128]{1,0:T(8,128)(2,1)} %get-tuple-element.41.pieces_ref), custom_call_target="tpu_custom_call" | custom-call | flops 1000000000 | bytes 1508388 | tf_op jit(solution)/shard_map/pallas_call | solution.py:56
  26.1 0.9 collective-permute-done.3.refs_12_.refs_10_
  27.5 1.0 collective-permute-done.7.refs_13_.refs_11_
  29.6 25.4 %shard_map.124 = (bf16[512,256]{1,0:T(8,128)(2,1)}, bf16[512,256]{1,0:T(8,128)(2,1)}, bf16[512,256]{1,0:T(8,128)(2,1)}) custom-call(s32[9]{0:T(128)} %get-tuple-element.44.refs_0_, f32[2048,128]{1,0:T(8,128)} %get-tuple-element.45.refs_1_, bf16[32,512,512]{2,1,0:T(8,128)(2,1)} %bitcast.16, bf16[512,256]{1,0:T(8,128)(2,1)} %get-tuple-element.46.refs_3_, ...), custom_call_target="tpu_custom_call" | custom-call | flops 17179869184 | bytes 23330852 | tf_op jit(solution)/shard_map/pallas_call | solution.py:56
  55.0 1.5 %collective-permute-start.10 = (bf16[512,256]{1,0:T(8,128)(2,1)}, bf16[512,256]{1,0:T(8,128)(2,1)S(1)}, u32[]{:S(2)}, u32[]{:S(2)}) collective-permute-start(bf16[512,256]{1,0:T(8,128)(2,1)} %get-tuple-element.51.refs_6_.refs_2_), channel_id=1, source_target_pairs={{0,8},{8,0},{16,24},{24,16},{1,9},{9,1},{17,25},{25,17},{2,10},{10... | collective-permute-start | bytes 786440 | tf_op jit(solution)/shard_map/ppermute | solution.py:405
  56.4 1.5 %collective-permute-start.11 = (bf16[512,256]{1,0:T(8,128)(2,1)}, bf16[512,256]{1,0:T(8,128)(2,1)S(1)}, u32[]{:S(2)}, u32[]{:S(2)}) collective-permute-start(bf16[512,256]{1,0:T(8,128)(2,1)} %get-tuple-element.51.refs_6_.refs_2_), channel_id=1, source_target_pairs={{0,2},{1,3},{2,0},{3,1},{4,6},{5,7},{6,4},{7,5},{8,10},{9,11},{10,... | collective-permute-start | bytes 786440 | tf_op jit(solution)/shard_map/ppermute | solution.py:405
  57.9 1.6 %collective-permute-start.12 = (bf16[512,256]{1,0:T(8,128)(2,1)}, bf16[512,256]{1,0:T(8,128)(2,1)S(1)}, u32[]{:S(2)}, u32[]{:S(2)}) collective-permute-start(bf16[512,256]{1,0:T(8,128)(2,1)} %get-tuple-element.51.refs_6_.refs_2_), channel_id=1, source_target_pairs={{0,4},{1,5},{2,6},{3,7},{4,0},{5,1},{6,2},{7,3},{8,12},{9,13},{10,... | collective-permute-start | bytes 786440 | tf_op jit(solution)/shard_map/ppermute | solution.py:405
  59.5 6.0 %shard_map.125 = (s32[8,8,4,256]{3,2,1,0:T(4,128)}, f32[8,8,1,256]{3,2,1,0:T(1,128)}, f32[2048,128]{1,0:T(8,128)}, s32[9]{0:T(128)}) custom-call(s32[32,8]{1,0:T(8,128)} %bitcast.11, s32[32,4,512]{2,1,0:T(4,128)} %copy-done.1, bf16[768,128]{1,0:T(8,128)(2,1)} %get-tuple-element.41.pieces_ref, bf16[48,128]{1,0:T(8,128)(2,1)} %get-tuple-element.52.own_ref), custom_call_target="tpu_custom_call" | custom-call | flops 1000000000 | bytes 1848356 | tf_op jit(solution)/shard_map/pallas_call | solution.py:56
  65.8 0.9 collective-permute-start.17
  66.8 1.1 collective-permute-start.18
  67.9 1.7 %collective-permute-start.19 = (bf16[512,256]{1,0:T(8,128)(2,1)S(1)}, bf16[512,256]{1,0:T(8,128)(2,1)S(1)}, u32[]{:S(2)}, u32[]{:S(2)}) collective-permute-start(bf16[512,256]{1,0:T(8,128)(2,1)S(1)} %collective-permute-done.12.refs_10_.refs_6_), channel_id=1, source_target_pairs={{0,2},{1,3},{2,0},{3,1},{4,6},{5,7},{6,4},{7,5},{8,10},{9,11},{10,... | collective-permute-start | bytes 786440 | tf_op jit(solution)/shard_map/ppermute | solution.py:405
  69.6 14.2 %shard_map.126.refs_0_ = bf16[4,512,512]{2,1,0:T(8,128)(2,1)} custom-call(s32[2]{0:T(128)} %pad_add_fusion.pos_ref.refs_0_, s32[8,8,4,256]{3,2,1,0:T(4,128)} %get-tuple-element.63.refs_1_, f32[8,8,1,256]{3,2,1,0:T(1,128)} %get-tuple-element.64.refs_2_, bf16[512,512]{1,0:T(8,128)(2,1)} %refs_3_.3, bf16[512,512]{1,0:T(8,128)(2,1)} %copy-done.24, ...), custom_call_target="tpu_custom_call" | custom-call | flops 8589934592 | bytes 6619144 | tf_op jit(solution)/shard_map/pallas_call | solution.py:56
  84.7 1.7 %collective-permute-start.9 = (bf16[512,256]{1,0:T(8,128)(2,1)S(1)}, bf16[512,256]{1,0:T(8,128)(2,1)S(1)}, u32[]{:S(2)}, u32[]{:S(2)}) collective-permute-start(bf16[512,256]{1,0:T(8,128)(2,1)S(1)} %copy-done.18), channel_id=1, source_target_pairs={{0,8},{8,0},{16,24},{24,16},{1,9},{9,1},{17,25},{25,17},{2,10},{10... | collective-permute-start | bytes 786440 | tf_op jit(solution)/shard_map/ppermute | solution.py:405
  86.4 3.9 %collective-permute-done.24.refs_20_.refs_16_ = bf16[512,256]{1,0:T(8,128)(2,1)S(1)} collective-permute-done((bf16[512,256]{1,0:T(8,128)(2,1)S(1)}, bf16[512,256]{1,0:T(8,128)(2,1)S(1)}, u32[]{:S(2)}, u32[]{:S(2)}) %collective-permute-start.24) | collective-permute-done | bytes 262176 | tf_op jit(solution)/shard_map/ppermute | solution.py:405
  90.3 14.3 %shard_map.127.refs_1_ = bf16[4,512,512]{2,1,0:T(8,128)(2,1)} custom-call(s32[2]{0:T(128)} %pad_add_fusion.pos_ref.refs_0_, s32[8,8,4,256]{3,2,1,0:T(4,128)} %get-tuple-element.63.refs_1_, f32[8,8,1,256]{3,2,1,0:T(1,128)} %get-tuple-element.64.refs_2_, bf16[512,512]{1,0:T(8,128)(2,1)} %refs_3_.3, bf16[512,512]{1,0:T(8,128)(2,1)} %copy-done.24, ...), custom_call_target="tpu_custom_call" | custom-call | flops 8589934592 | bytes 6619144 | tf_op jit(solution)/shard_map/pallas_call | solution.py:56
  106.4 0.7 constant_dynamic-slice_fusion.refs_3_
  107.1 1.1 broadcast_select_fusion.3
  109.2 0.7 copy-done.17
  109.9 25.6 %shard_map.128 = bf16[512,256]{1,0:T(8,128)(2,1)} custom-call(s32[9]{0:T(128)} %get-tuple-element.57.refs_0_, f32[2048,128]{1,0:T(8,128)} %get-tuple-element.58.refs_1_, bf16[32,512,512]{2,1,0:T(8,128)(2,1)} %bitcast.17, bf16[256,512]{1,0:T(8,128)(2,1)} %constant_dynamic-slice_fusion.refs_3_, bf16[512,256]{1,0:T(8,128)(2,1)} %get-tuple-element.59.refs_4_, ...), custom_call_target="tpu_custom_call" | custom-call | flops 17179869184 | bytes 23068708 | tf_op jit(solution)/shard_map/pallas_call | solution.py:56
  135.9 0.8 pad_maximum_fusion
  136.7 7.8 %shard_map.129 = f32[512,512]{1,0:T(8,128)} custom-call(bf16[4,512,512]{2,1,0:T(8,128)(2,1)} %shard_map.126.refs_0_, bf16[4,512,512]{2,1,0:T(8,128)(2,1)} %shard_map.127.refs_1_, bf16[512,256]{1,0:T(8,128)(2,1)} %get-tuple-element.51.refs_6_.refs_2_, bf16[512,256]{1,0:T(8,128)(2,1)} %copy-done.10, bf16[512,256]{1,0:T(8,128)(2,1)} %copy-done.4, ...), custom_call_target="tpu_custom_call" | custom-call | flops 2147483648 | bytes 9437184 | tf_op jit(solution)/shard_map/pallas_call | solution.py:56
  144.6 0.8 pad_maximum_fusion.1
  (106 shorter events, 7.8 us)
Async XLA Ops:
  0.6 16.8 %collective-permute-start = (bf16[512,512]{1,0:T(8,128)(2,1)}, bf16[512,512]{1,0:T(8,128)(2,1)S(1)}, u32[]{:S(2)}, u32[]{:S(2)}) collective-permute-start(bf16[512,512]{1,0:T(8,128)(2,1)} %refs_3_.3), channel_id=1, source_target_pairs={{0,2},{1,3},{2,0},{3,1},{4,6},{5,7},{6,4},{7,5},{8,10},{9,11},{10,... | collective-permute-start | bytes 1572872 | tf_op jit(solution)/shard_map/ppermute | solution.py:405
  3.6 15.6 %collective-permute-start.1 = (bf16[512,512]{1,0:T(8,128)(2,1)}, bf16[512,512]{1,0:T(8,128)(2,1)S(1)}, u32[]{:S(2)}, u32[]{:S(2)}) collective-permute-start(bf16[512,512]{1,0:T(8,128)(2,1)} %refs_3_.3), channel_id=1, source_target_pairs={{0,4},{1,5},{2,6},{3,7},{4,0},{5,1},{6,2},{7,3},{8,12},{9,13},{10,... | collective-permute-start | bytes 1572872 | tf_op jit(solution)/shard_map/ppermute | solution.py:405
  7.0 15.0 %all-to-all-start = ((s32[32,4,512]{2,1,0:T(4,128)}), s32[32,4,512]{2,1,0:T(4,128)S(1)}, u32[]{:S(2)}, u32[]{:S(2)}) async-start(s32[32,4,512]{2,1,0:T(4,128)} %shard_map.122), calls=%async_computation | async-start | bytes 524288 | tf_op jit(solution)/shard_map/all_to_all | solution.py:473
  19.3 6.8 %collective-permute-start.2 = (bf16[256,512]{1,0:T(8,128)(2,1)S(1)}, bf16[256,512]{1,0:T(8,128)(2,1)S(1)}, u32[]{:S(2)}, u32[]{:S(2)}) collective-permute-start(bf16[256,512]{1,0:T(8,128)(2,1)S(1)} %slice.9), channel_id=1, source_target_pairs={{0,2},{1,3},{2,0},{3,1},{4,6},{5,7},{6,4},{7,5},{8,10},{9,11},{10,... | collective-permute-start | bytes 786440 | tf_op jit(solution)/shard_map/ppermute | solution.py:405
  19.4 7.6 %collective-permute-start.3 = (bf16[256,512]{1,0:T(8,128)(2,1)S(1)}, bf16[256,512]{1,0:T(8,128)(2,1)S(1)}, u32[]{:S(2)}, u32[]{:S(2)}) collective-permute-start(bf16[256,512]{1,0:T(8,128)(2,1)S(1)} %slice.10), channel_id=1, source_target_pairs={{0,4},{1,5},{2,6},{3,7},{4,0},{5,1},{6,2},{7,3},{8,12},{9,13},{10,... | collective-permute-start | bytes 786440 | tf_op jit(solution)/shard_map/ppermute | solution.py:405
  21.5 6.0 %collective-permute-start.4 = (bf16[512,512]{1,0:T(8,128)(2,1)S(1)}, bf16[512,512]{1,0:T(8,128)(2,1)S(1)}, u32[]{:S(2)}, u32[]{:S(2)}) collective-permute-start(bf16[512,512]{1,0:T(8,128)(2,1)S(1)} %copy-done.23), channel_id=1, source_target_pairs={{0,1},{1,0},{2,3},{3,2},{4,5},{5,4},{6,7},{7,6},{8,9},{9,8},{10,11... | collective-permute-start | bytes 1572872 | tf_op jit(solution)/shard_map/ppermute | solution.py:405
  21.5 7.4 %collective-permute-start.5 = (bf16[512,512]{1,0:T(8,128)(2,1)S(1)}, bf16[512,512]{1,0:T(8,128)(2,1)}, u32[]{:S(2)}, u32[]{:S(2)}) collective-permute-start(bf16[512,512]{1,0:T(8,128)(2,1)S(1)} %collective-permute-done.refs_7_.refs_5_), channel_id=1, source_target_pairs={{0,1},{1,0},{2,3},{3,2},{4,5},{5,4},{6,7},{7,6},{8,9},{9,8},{10,11... | collective-permute-start | bytes 1572872 | tf_op jit(solution)/shard_map/ppermute | solution.py:405
  22.0 6.9 %collective-permute-start.6 = (bf16[512,512]{1,0:T(8,128)(2,1)S(1)}, bf16[512,512]{1,0:T(8,128)(2,1)}, u32[]{:S(2)}, u32[]{:S(2)}) collective-permute-start(bf16[512,512]{1,0:T(8,128)(2,1)S(1)} %collective-permute-done.1.refs_9_.refs_7_), channel_id=1, source_target_pairs={{0,1},{1,0},{2,3},{3,2},{4,5},{5,4},{6,7},{7,6},{8,9},{9,8},{10,11... | collective-permute-start | bytes 1572872 | tf_op jit(solution)/shard_map/ppermute | solution.py:405
  27.0 1.5 %collective-permute-start.7 = (bf16[256,512]{1,0:T(8,128)(2,1)S(1)}, bf16[256,512]{1,0:T(8,128)(2,1)S(1)}, u32[]{:S(2)}, u32[]{:S(2)}) collective-permute-start(bf16[256,512]{1,0:T(8,128)(2,1)S(1)} %collective-permute-done.2.refs_11_.refs_9_), channel_id=1, source_target_pairs={{0,1},{1,0},{2,3},{3,2},{4,5},{5,4},{6,7},{7,6},{8,9},{9,8},{10,11... | collective-permute-start | bytes 786440 | tf_op jit(solution)/shard_map/ppermute | solution.py:405
  27.0 1.9 %collective-permute-start.8 = (bf16[256,512]{1,0:T(8,128)(2,1)S(1)}, bf16[256,512]{1,0:T(8,128)(2,1)S(1)}, u32[]{:S(2)}, u32[]{:S(2)}) collective-permute-start(bf16[256,512]{1,0:T(8,128)(2,1)S(1)} %collective-permute-done.3.refs_12_.refs_10_), channel_id=1, source_target_pairs={{0,1},{1,0},{2,3},{3,2},{4,5},{5,4},{6,7},{7,6},{8,9},{9,8},{10,11... | collective-permute-start | bytes 786440 | tf_op jit(solution)/shard_map/ppermute | solution.py:405
  55.0 10.6 %collective-permute-start.10 = (bf16[512,256]{1,0:T(8,128)(2,1)}, bf16[512,256]{1,0:T(8,128)(2,1)S(1)}, u32[]{:S(2)}, u32[]{:S(2)}) collective-permute-start(bf16[512,256]{1,0:T(8,128)(2,1)} %get-tuple-element.51.refs_6_.refs_2_), channel_id=1, source_target_pairs={{0,8},{8,0},{16,24},{24,16},{1,9},{9,1},{17,25},{25,17},{2,10},{10... | collective-permute-start | bytes 786440 | tf_op jit(solution)/shard_map/ppermute | solution.py:405
  56.4 9.1 %collective-permute-start.11 = (bf16[512,256]{1,0:T(8,128)(2,1)}, bf16[512,256]{1,0:T(8,128)(2,1)S(1)}, u32[]{:S(2)}, u32[]{:S(2)}) collective-permute-start(bf16[512,256]{1,0:T(8,128)(2,1)} %get-tuple-element.51.refs_6_.refs_2_), channel_id=1, source_target_pairs={{0,2},{1,3},{2,0},{3,1},{4,6},{5,7},{6,4},{7,5},{8,10},{9,11},{10,... | collective-permute-start | bytes 786440 | tf_op jit(solution)/shard_map/ppermute | solution.py:405
  57.9 7.9 %collective-permute-start.12 = (bf16[512,256]{1,0:T(8,128)(2,1)}, bf16[512,256]{1,0:T(8,128)(2,1)S(1)}, u32[]{:S(2)}, u32[]{:S(2)}) collective-permute-start(bf16[512,256]{1,0:T(8,128)(2,1)} %get-tuple-element.51.refs_6_.refs_2_), channel_id=1, source_target_pairs={{0,4},{1,5},{2,6},{3,7},{4,0},{5,1},{6,2},{7,3},{8,12},{9,13},{10,... | collective-permute-start | bytes 786440 | tf_op jit(solution)/shard_map/ppermute | solution.py:405
  65.5 39.1 %copy-start.3 = (bf16[512,256]{1,0:T(8,128)(2,1)}, bf16[512,256]{1,0:T(8,128)(2,1)S(1)}, u32[]{:S(2)}) copy-start(bf16[512,256]{1,0:T(8,128)(2,1)S(1)} %collective-permute-done.10.refs_14_.refs_10_) | copy-start | bytes 786436
  65.6 24.7 %copy-start.4 = (bf16[512,256]{1,0:T(8,128)(2,1)}, bf16[512,256]{1,0:T(8,128)(2,1)S(1)}, u32[]{:S(2)}) copy-start(bf16[512,256]{1,0:T(8,128)(2,1)S(1)} %collective-permute-done.11.refs_8_.refs_4_) | copy-start | bytes 786436
  65.8 18.0 %collective-permute-start.17 = (bf16[512,256]{1,0:T(8,128)(2,1)S(1)}, bf16[512,256]{1,0:T(8,128)(2,1)S(1)}, u32[]{:S(2)}, u32[]{:S(2)}) collective-permute-start(bf16[512,256]{1,0:T(8,128)(2,1)S(1)} %collective-permute-done.10.refs_14_.refs_10_), channel_id=1, source_target_pairs={{0,2},{1,3},{2,0},{3,1},{4,6},{5,7},{6,4},{7,5},{8,10},{9,11},{10,... | collective-permute-start | bytes 786440 | tf_op jit(solution)/shard_map/ppermute | solution.py:405
  66.8 17.1 %collective-permute-start.18 = (bf16[512,256]{1,0:T(8,128)(2,1)S(1)}, bf16[512,256]{1,0:T(8,128)(2,1)S(1)}, u32[]{:S(2)}, u32[]{:S(2)}) collective-permute-start(bf16[512,256]{1,0:T(8,128)(2,1)S(1)} %collective-permute-done.10.refs_14_.refs_10_), channel_id=1, source_target_pairs={{0,4},{1,5},{2,6},{3,7},{4,0},{5,1},{6,2},{7,3},{8,12},{9,13},{10,... | collective-permute-start | bytes 786440 | tf_op jit(solution)/shard_map/ppermute | solution.py:405
  67.9 15.9 %collective-permute-start.19 = (bf16[512,256]{1,0:T(8,128)(2,1)S(1)}, bf16[512,256]{1,0:T(8,128)(2,1)S(1)}, u32[]{:S(2)}, u32[]{:S(2)}) collective-permute-start(bf16[512,256]{1,0:T(8,128)(2,1)S(1)} %collective-permute-done.12.refs_10_.refs_6_), channel_id=1, source_target_pairs={{0,2},{1,3},{2,0},{3,1},{4,6},{5,7},{6,4},{7,5},{8,10},{9,11},{10,... | collective-permute-start | bytes 786440 | tf_op jit(solution)/shard_map/ppermute | solution.py:405
  83.8 21.9 %copy-start.7 = (bf16[512,256]{1,0:T(8,128)(2,1)}, bf16[512,256]{1,0:T(8,128)(2,1)S(1)}, u32[]{:S(2)}) copy-start(bf16[512,256]{1,0:T(8,128)(2,1)S(1)} %collective-permute-done.18.refs_18_.refs_14_) | copy-start | bytes 786436
  83.9 6.4 %collective-permute-start.24 = (bf16[512,256]{1,0:T(8,128)(2,1)S(1)}, bf16[512,256]{1,0:T(8,128)(2,1)S(1)}, u32[]{:S(2)}, u32[]{:S(2)}) collective-permute-start(bf16[512,256]{1,0:T(8,128)(2,1)S(1)} %collective-permute-done.17.refs_16_.refs_12_), channel_id=1, source_target_pairs={{0,4},{1,5},{2,6},{3,7},{4,0},{5,1},{6,2},{7,3},{8,12},{9,13},{10,... | collective-permute-start | bytes 786440 | tf_op jit(solution)/shard_map/ppermute | solution.py:405
  84.2 20.4 %collective-permute-start.14 = (bf16[512,256]{1,0:T(8,128)(2,1)S(1)}, bf16[512,256]{1,0:T(8,128)(2,1)S(1)}, u32[]{:S(2)}, u32[]{:S(2)}) collective-permute-start(bf16[512,256]{1,0:T(8,128)(2,1)S(1)} %copy-done.2), channel_id=1, source_target_pairs={{0,1},{1,0},{2,3},{3,2},{4,5},{5,4},{6,7},{7,6},{8,9},{9,8},{10,11... | collective-permute-start | bytes 786440 | tf_op jit(solution)/shard_map/ppermute | solution.py:405
  84.3 20.9 %collective-permute-start.13 = (bf16[512,256]{1,0:T(8,128)(2,1)S(1)}, bf16[512,256]{1,0:T(8,128)(2,1)S(1)}, u32[]{:S(2)}, u32[]{:S(2)}) collective-permute-start(bf16[512,256]{1,0:T(8,128)(2,1)S(1)} %copy-done.25), channel_id=1, source_target_pairs={{0,8},{8,0},{16,24},{24,16},{1,9},{9,1},{17,25},{25,17},{2,10},{10... | collective-permute-start | bytes 786440 | tf_op jit(solution)/shard_map/ppermute | solution.py:405
  84.7 21.7 %copy-start = (bf16[512,512]{1,0:T(8,128)(2,1)S(1)}, bf16[512,512]{1,0:T(8,128)(2,1)}, u32[]{:S(2)}) copy-start(bf16[512,512]{1,0:T(8,128)(2,1)} %param.11) | copy-start | bytes 1572868
  84.7 20.6 %collective-permute-start.9 = (bf16[512,256]{1,0:T(8,128)(2,1)S(1)}, bf16[512,256]{1,0:T(8,128)(2,1)S(1)}, u32[]{:S(2)}, u32[]{:S(2)}) collective-permute-start(bf16[512,256]{1,0:T(8,128)(2,1)S(1)} %copy-done.18), channel_id=1, source_target_pairs={{0,8},{8,0},{16,24},{24,16},{1,9},{9,1},{17,25},{25,17},{2,10},{10... | collective-permute-start | bytes 786440 | tf_op jit(solution)/shard_map/ppermute | solution.py:405
  86.4 19.6 %collective-permute-start.16 = (bf16[512,256]{1,0:T(8,128)(2,1)S(1)}, bf16[512,256]{1,0:T(8,128)(2,1)S(1)}, u32[]{:S(2)}, u32[]{:S(2)}) collective-permute-start(bf16[512,256]{1,0:T(8,128)(2,1)S(1)} %collective-permute-done.12.refs_10_.refs_6_), channel_id=1, source_target_pairs={{0,1},{1,0},{2,3},{3,2},{4,5},{5,4},{6,7},{7,6},{8,9},{9,8},{10,11... | collective-permute-start | bytes 786440 | tf_op jit(solution)/shard_map/ppermute | solution.py:405
  90.3 15.5 %collective-permute-start.15 = (bf16[512,256]{1,0:T(8,128)(2,1)S(1)}, bf16[512,256]{1,0:T(8,128)(2,1)S(1)}, u32[]{:S(2)}, u32[]{:S(2)}) collective-permute-start(bf16[512,256]{1,0:T(8,128)(2,1)S(1)} %collective-permute-done.11.refs_8_.refs_4_), channel_id=1, source_target_pairs={{0,1},{1,0},{2,3},{3,2},{4,5},{5,4},{6,7},{7,6},{8,9},{9,8},{10,11... | collective-permute-start | bytes 786440 | tf_op jit(solution)/shard_map/ppermute | solution.py:405
  104.6 3.6 %collective-permute-start.21 = (bf16[512,256]{1,0:T(8,128)(2,1)S(1)}, bf16[512,256]{1,0:T(8,128)(2,1)S(1)}, u32[]{:S(2)}, u32[]{:S(2)}) collective-permute-start(bf16[512,256]{1,0:T(8,128)(2,1)S(1)} %collective-permute-done.10.refs_14_.refs_10_), channel_id=1, source_target_pairs={{0,1},{1,0},{2,3},{3,2},{4,5},{5,4},{6,7},{7,6},{8,9},{9,8},{10,11... | collective-permute-start | bytes 786440 | tf_op jit(solution)/shard_map/ppermute | solution.py:405
  105.1 3.1 %collective-permute-start.22 = (bf16[512,256]{1,0:T(8,128)(2,1)S(1)}, bf16[512,256]{1,0:T(8,128)(2,1)S(1)}, u32[]{:S(2)}, u32[]{:S(2)}) collective-permute-start(bf16[512,256]{1,0:T(8,128)(2,1)S(1)} %collective-permute-done.17.refs_16_.refs_12_), channel_id=1, source_target_pairs={{0,1},{1,0},{2,3},{3,2},{4,5},{5,4},{6,7},{7,6},{8,9},{9,8},{10,11... | collective-permute-start | bytes 786440 | tf_op jit(solution)/shard_map/ppermute | solution.py:405
  105.3 2.9 %collective-permute-start.20 = (bf16[512,256]{1,0:T(8,128)(2,1)S(1)}, bf16[512,256]{1,0:T(8,128)(2,1)S(1)}, u32[]{:S(2)}, u32[]{:S(2)}) collective-permute-start(bf16[512,256]{1,0:T(8,128)(2,1)S(1)} %collective-permute-done.19.refs_12_.refs_8_), channel_id=1, source_target_pairs={{0,1},{1,0},{2,3},{3,2},{4,5},{5,4},{6,7},{7,6},{8,9},{9,8},{10,11... | collective-permute-start | bytes 786440 | tf_op jit(solution)/shard_map/ppermute | solution.py:405
  105.8 2.5 %collective-permute-start.23 = (bf16[512,256]{1,0:T(8,128)(2,1)S(1)}, bf16[512,256]{1,0:T(8,128)(2,1)S(1)}, u32[]{:S(2)}, u32[]{:S(2)}) collective-permute-start(bf16[512,256]{1,0:T(8,128)(2,1)S(1)} %collective-permute-done.18.refs_18_.refs_14_), channel_id=1, source_target_pairs={{0,1},{1,0},{2,3},{3,2},{4,5},{5,4},{6,7},{7,6},{8,9},{9,8},{10,11... | collective-permute-start | bytes 786440 | tf_op jit(solution)/shard_map/ppermute | solution.py:405
  105.9 2.4 %collective-permute-start.25 = (bf16[512,256]{1,0:T(8,128)(2,1)S(1)}, bf16[512,256]{1,0:T(8,128)(2,1)S(1)}, u32[]{:S(2)}, u32[]{:S(2)}) collective-permute-start(bf16[512,256]{1,0:T(8,128)(2,1)S(1)} %collective-permute-done.24.refs_20_.refs_16_), channel_id=1, source_target_pairs={{0,1},{1,0},{2,3},{3,2},{4,5},{5,4},{6,7},{7,6},{8,9},{9,8},{10,11... | collective-permute-start | bytes 786440 | tf_op jit(solution)/shard_map/ppermute | solution.py:405
  135.5 9.1 %collective-permute-start.26 = (bf16[512,256]{1,0:T(8,128)(2,1)}, bf16[512,256]{1,0:T(8,128)(2,1)S(1)}, u32[]{:S(2)}, u32[]{:S(2)}) collective-permute-start(bf16[512,256]{1,0:T(8,128)(2,1)} %shard_map.128), channel_id=1, source_target_pairs={{0,8},{8,0},{16,24},{24,16},{1,9},{9,1},{17,25},{25,17},{2,10},{10... | collective-permute-start | bytes 786440 | tf_op jit(solution)/shard_map/ppermute | solution.py:405
  (27 other events, 202.1 us)
